TPU v7x, 256 devices: a whole 4x4x8 slice. The times are simulated.
256 devices in a mesh: dp: 64 (over z, y, core), mp: 4 (over x).
Axes of the slice: x: 4, y: 4, z: 8, core: 2. Of those that a mesh axis runs over, the one named last changes fastest.
Arguments:
- tokens: bfloat16 [131072, 1024], P('dp'), may hold values from -96 to 96
- doc_ids: int32 [131072], P('dp'), may hold values from 0 to 2047, as said below
- ln_gain: float32 [1024], replicated, may hold values from 0.1 to 1.9
- w_query: bfloat16 [1024, 1024], P(None, 'mp'), may hold values from -16 to 16
- w_key: bfloat16 [1024, 1024], P(None, 'mp'), may hold values from -0.5 to 0.5
- w_value: bfloat16 [1024, 1024], P(None, 'mp'), may hold values from -0.1875 to 0.1875
- w_out: bfloat16 [1024, 1024], P('mp'), may hold values from -0.1875 to 0.1875
- centroids: float32 [65536, 1024], P('dp', 'mp'), may hold values from -6 to 6
- cluster_mass: float32 [65536], P('dp'), may hold values from 0.5 to 4
- assigned: int32 [2048], P('dp'), may hold values from 0 to 65535, as said below
Outputs:
- doc_vectors: float32 [2048, 1024], P('dp', 'mp')
- new_centroids: float32 [65536, 1024], P('dp', 'mp')
Inputs may be any that keep to these rules, and one draw needn't show every extreme that they name: `doc_ids`: never falls along the positions. The documents that begin in row r (positions r * 2048 onward) have the ids r * 32 upward without gaps, from 24 to 32 of them, and some row has 32; ids of slots that no document takes never occur. A row begins with its own first document or with the rest of the last document begun in the row before, and row 0 begins with document 0; every document lies within the row where it begins and the next one. `assigned`: centroid c belongs to dp index c // 1024. Among the 32 slots of one row at most 2 name centroids of one dp index; in every row exactly 2 slots that hold documents name centroids of one dp index common to all rows.
All inputs are finite; a program needn't handle non-finite values.
Results may differ from a plain program's by a relative error of at most 0.0024.
Values sent between devices are 32-bit elements; how exact they have to be, the bound alone decides.
A program may use at most 128 MiB of HBM per device.

v0:
```python
import math

import jax
import jax.numpy as jnp
from jax import lax
from jax.sharding import PartitionSpec as P

D = 1024
HEAD_DIM = 64


def shifted(x, axis, by):
    devices = lax.axis_size(axis)
    pairs = [(i, i + by) for i in range(devices) if 0 <= i + by < devices]
    return lax.ppermute(x, axis, pairs)


def layer_norm(tokens, ln_gain):
    widened = tokens.astype(jnp.float32)
    average = jnp.mean(widened, axis=-1, keepdims=True)
    centered = widened - average
    variance = jnp.mean(centered * centered, axis=-1, keepdims=True)
    return (centered * lax.rsqrt(variance + 1e-05) * ln_gain).astype(jnp.bfloat16)


def attend_block(queries, keys_all, values_all, query_ids, row_ids):
    scores = jnp.einsum("qhd,khd->hqk", queries, keys_all, preferred_element_type=jnp.float32) * (
        1.0 / math.sqrt(HEAD_DIM)
    )
    same_doc = query_ids[:, None] == row_ids[None, :]
    scores = jnp.where(same_doc[None], scores, -1e30)
    top_score = jnp.max(scores, axis=-1, keepdims=True)
    raised = jnp.exp(scores - top_score)
    weights = (raised / jnp.sum(raised, axis=-1, keepdims=True)).astype(jnp.bfloat16)
    return jnp.einsum(
        "hqk,khd->qhd", weights, values_all, preferred_element_type=jnp.float32
    ).astype(jnp.bfloat16)


def self_attention(normed, w_query, w_key, w_value, row_ids):
    length = normed.shape[0]
    width = w_query.shape[1]
    head_count = width // HEAD_DIM

    def project(weight):
        return (
            jnp.dot(normed, weight, preferred_element_type=jnp.float32)
            .astype(jnp.bfloat16)
            .reshape(length, head_count, HEAD_DIM)
        )

    queries = project(w_query)
    keys_all = project(w_key)
    values_all = project(w_value)
    block_rows = min(512, length)
    query_blocks = queries.reshape(length // block_rows, block_rows, head_count, HEAD_DIM)
    id_blocks = row_ids.reshape(length // block_rows, block_rows)
    context = lax.map(
        lambda pair: attend_block(pair[0], keys_all, values_all, pair[1], row_ids),
        (query_blocks, id_blocks),
    )
    return context.reshape(length, width)


def shards(
    tokens, doc_ids, ln_gain, w_query, w_key, w_value, w_out, centroids, cluster_mass, assigned
):
    length = tokens.shape[0]
    slot_count = assigned.shape[0]
    local_width = w_out.shape[0]
    cent_count = centroids.shape[0]
    row_index = lax.axis_index("dp")
    column_start = lax.axis_index("mp") * local_width
    highest = lax.Precision.HIGHEST
    dp_count = lax.axis_size("dp")
    capacity = max(2, (slot_count + dp_count - 2) // (dp_count - 1))
    normed = layer_norm(tokens, ln_gain)
    context = self_attention(normed, w_query, w_key, w_value, doc_ids)
    local_slot = doc_ids - row_index * slot_count
    targets = jnp.where(local_slot < 0, slot_count, local_slot)
    member = jnp.arange(slot_count + 1, dtype=jnp.int32)[:, None] == targets[None, :]
    counts = jnp.sum(member.astype(jnp.float32), axis=1)
    own_columns = lax.dynamic_slice_in_dim(tokens, column_start, local_width, 1)
    partial_out = jnp.dot(context, w_out, preferred_element_type=jnp.float32)
    mixed = own_columns.astype(jnp.float32) + lax.psum_scatter(
        partial_out, "mp", scatter_dimension=1, tiled=True
    )
    pooled = jnp.dot(member.astype(jnp.float32), mixed, precision=highest)
    received_sum, received_count = shifted((pooled[slot_count:], counts[slot_count:]), "dp", -1)
    last_pick = (jnp.arange(slot_count, dtype=jnp.int32) == local_slot[length - 1]).astype(
        jnp.float32
    )
    doc_sums = pooled[:slot_count] + last_pick[:, None] * received_sum
    doc_counts = counts[:slot_count] + last_pick * received_count[0]
    averages = doc_sums / jnp.maximum(doc_counts, 1.0)[:, None]
    squares = lax.psum(jnp.sum(averages * averages, axis=1), "mp")
    doc_vectors = averages * lax.rsqrt(squares / D + 1e-06)[:, None]
    is_used = doc_counts > 0
    gathered, all_assigned, all_used = (
        lax.all_gather(doc_vectors, "dp", axis=0, tiled=True),
        lax.all_gather(assigned.astype(jnp.float32), "dp", axis=0, tiled=True),
        lax.all_gather(is_used.astype(jnp.float32), "dp", axis=0, tiled=True),
    )
    offset = all_assigned - (row_index * cent_count).astype(jnp.float32)
    is_mine = (all_used > 0) & (offset >= 0) & (offset < cent_count)
    kept_total = dp_count * capacity
    picked = jnp.nonzero(is_mine, size=kept_total, fill_value=0)[0].astype(jnp.int32)
    kept_count = jnp.sum(is_mine.astype(jnp.int32))
    valid_slot = jnp.arange(kept_total, dtype=jnp.int32) < kept_count
    arriving = jnp.take(gathered, picked, axis=0)
    target = jnp.where(valid_slot, jnp.take(offset, picked, axis=0), -1.0)
    hits_table = (
        jnp.arange(cent_count, dtype=jnp.int32).astype(jnp.float32)[:, None] == target[None, :]
    ).astype(jnp.float32)
    gained = jnp.dot(hits_table, arriving, precision=highest)
    members = jnp.sum(hits_table, axis=1)
    blended = cluster_mass[:, None] * centroids + gained
    norm_terms = lax.psum(jnp.sum(blended * blended, axis=1), "mp")
    scaled = blended * lax.rsqrt(norm_terms / D + 1e-06)[:, None]
    updated = jnp.where((members > 0)[:, None], scaled, centroids)
    return (doc_vectors, updated)


def solution(mesh):
    placed = (
        P("dp", None),
        P("dp"),
        P(),
        P(None, "mp"),
        P(None, "mp"),
        P(None, "mp"),
        P("mp", None),
        P("dp", "mp"),
        P("dp"),
        P("dp"),
    )
    return jax.shard_map(
        shards,
        mesh=mesh,
        in_specs=placed,
        out_specs=(P("dp", "mp"), P("dp", "mp")),
        check_vma=False,
    )
```

profile of v0, /device:TPU:1, one launch (start us, length us, event | category | flops | bytes accessed | tf_op | source)
XLA Modules:
  0.0 507.1 jit_solution(15355426650116754522)
XLA Ops:
  7.2 0.0 reduce-scatter.2.cloned.1.call-start
  7.3 3.0 convert_reduce_fusion
  10.2 0.5 copy-done.1
  10.7 1.4 fusion.30
  12.2 2.7 fusion.32
  14.9 4.4 convolution_convert_fusion.2
  19.3 3.4 reshape.271
  22.7 2.3 copy.25
  25.0 4.6 convolution_convert_fusion.1
  29.6 4.6 convolution_convert_fusion
  34.1 79.7 %while.10 = (s32[]{:T(128)}, bf16[4,512,4,64]{1,3,2,0:T(8,128)(2,1)S(1)}, s32[4,512]{1,0:T(4,128)S(1)}, s32[2048]{0:T(1024)S(1)}, bf16[4,512,4,64]{1,3,2,0:T(8,1...) while((s32[]{:T(128)}, bf16[4,512,4,64]{1,3,2,0:T(8,128)(2,1)S(1)}, ...), condition=%wide.region_5.6_spmd, body=%wide.region_2.5_spmd.sunk | while | flops 1100089344 | bytes 38304348 | solution.py:58
  34.4 0.7 broadcast_compare_fusion.3
  35.0 10.5 %fusion.82 = (f32[4,512]{1,0:T(4,128)S(1)}, f32[4,512,2048]{2,1,0:T(8,128)}) fusion(pred[512,2048]{1,0:T(8,128)(4,1)S(1)} %broadcast_compare_fusion.3, bf16[2048,4,64]{0,2,1:T(8,128)(2,1)} %get-tuple-element.166, bf16[4,512,4,64]{1,3,2,0:T(8,128)(2,1)} %get-tuple-element.165, s32[]{:T(128)} %get-tuple-element.153), kind=kOutput, calls=%fused_computation.102.clone.1 | convolution fusion | flops 553650176 | bytes 19145216 | tf_op jit(solution)/shard_map/while/body/eval_jaxpr/sub | solution.py:33
  45.5 8.7 %fusion.83 = bf16[4,512,4,64]{1,3,2,0:T(8,128)(2,1)S(1)} fusion(bf16[4,512,4,64]{1,3,2,0:T(8,128)(2,1)S(1)} %get-tuple-element.154, s32[]{:T(128)} %get-tuple-element.153, bf16[2048,4,64]{0,2,1:T(8,128)(2,1)} %get-tuple-element.167, f32[4,512,2048]{2,1,0:T(8,128)} %get-tuple-element.143, f32[4,512]{1,0:T(4,128)S(1)} %get-tuple-element.144), kind=kOutput, calls=%fused_computation.16.clone.1 | convolution fusion | flops 545390592 | bytes 18096132 | tf_op jit(solution)/shard_map/while/body/eval_jaxpr/hqk,khd->qhd/dot_general | solution.py:35
  54.2 0.7 broadcast_compare_fusion.3
  54.9 10.5 %fusion.82 = (f32[4,512]{1,0:T(4,128)S(1)}, f32[4,512,2048]{2,1,0:T(8,128)}) fusion(pred[512,2048]{1,0:T(8,128)(4,1)S(1)} %broadcast_compare_fusion.3, bf16[2048,4,64]{0,2,1:T(8,128)(2,1)} %get-tuple-element.166, bf16[4,512,4,64]{1,3,2,0:T(8,128)(2,1)} %get-tuple-element.165, s32[]{:T(128)} %get-tuple-element.153), kind=kOutput, calls=%fused_computation.102.clone.1 | convolution fusion | flops 553650176 | bytes 19145216 | tf_op jit(solution)/shard_map/while/body/eval_jaxpr/sub | solution.py:33
  65.4 8.7 %fusion.83 = bf16[4,512,4,64]{1,3,2,0:T(8,128)(2,1)S(1)} fusion(bf16[4,512,4,64]{1,3,2,0:T(8,128)(2,1)S(1)} %get-tuple-element.154, s32[]{:T(128)} %get-tuple-element.153, bf16[2048,4,64]{0,2,1:T(8,128)(2,1)} %get-tuple-element.167, f32[4,512,2048]{2,1,0:T(8,128)} %get-tuple-element.143, f32[4,512]{1,0:T(4,128)S(1)} %get-tuple-element.144), kind=kOutput, calls=%fused_computation.16.clone.1 | convolution fusion | flops 545390592 | bytes 18096132 | tf_op jit(solution)/shard_map/while/body/eval_jaxpr/hqk,khd->qhd/dot_general | solution.py:35
  74.1 0.7 broadcast_compare_fusion.3
  74.8 10.5 %fusion.82 = (f32[4,512]{1,0:T(4,128)S(1)}, f32[4,512,2048]{2,1,0:T(8,128)}) fusion(pred[512,2048]{1,0:T(8,128)(4,1)S(1)} %broadcast_compare_fusion.3, bf16[2048,4,64]{0,2,1:T(8,128)(2,1)} %get-tuple-element.166, bf16[4,512,4,64]{1,3,2,0:T(8,128)(2,1)} %get-tuple-element.165, s32[]{:T(128)} %get-tuple-element.153), kind=kOutput, calls=%fused_computation.102.clone.1 | convolution fusion | flops 553650176 | bytes 19145216 | tf_op jit(solution)/shard_map/while/body/eval_jaxpr/sub | solution.py:33
  85.2 8.7 %fusion.83 = bf16[4,512,4,64]{1,3,2,0:T(8,128)(2,1)S(1)} fusion(bf16[4,512,4,64]{1,3,2,0:T(8,128)(2,1)S(1)} %get-tuple-element.154, s32[]{:T(128)} %get-tuple-element.153, bf16[2048,4,64]{0,2,1:T(8,128)(2,1)} %get-tuple-element.167, f32[4,512,2048]{2,1,0:T(8,128)} %get-tuple-element.143, f32[4,512]{1,0:T(4,128)S(1)} %get-tuple-element.144), kind=kOutput, calls=%fused_computation.16.clone.1 | convolution fusion | flops 545390592 | bytes 18096132 | tf_op jit(solution)/shard_map/while/body/eval_jaxpr/hqk,khd->qhd/dot_general | solution.py:35
  94.0 0.7 broadcast_compare_fusion.3
  94.6 10.5 %fusion.82 = (f32[4,512]{1,0:T(4,128)S(1)}, f32[4,512,2048]{2,1,0:T(8,128)}) fusion(pred[512,2048]{1,0:T(8,128)(4,1)S(1)} %broadcast_compare_fusion.3, bf16[2048,4,64]{0,2,1:T(8,128)(2,1)} %get-tuple-element.166, bf16[4,512,4,64]{1,3,2,0:T(8,128)(2,1)} %get-tuple-element.165, s32[]{:T(128)} %get-tuple-element.153), kind=kOutput, calls=%fused_computation.102.clone.1 | convolution fusion | flops 553650176 | bytes 19145216 | tf_op jit(solution)/shard_map/while/body/eval_jaxpr/sub | solution.py:33
  105.1 8.7 %fusion.83 = bf16[4,512,4,64]{1,3,2,0:T(8,128)(2,1)S(1)} fusion(bf16[4,512,4,64]{1,3,2,0:T(8,128)(2,1)S(1)} %get-tuple-element.154, s32[]{:T(128)} %get-tuple-element.153, bf16[2048,4,64]{0,2,1:T(8,128)(2,1)} %get-tuple-element.167, f32[4,512,2048]{2,1,0:T(8,128)} %get-tuple-element.143, f32[4,512]{1,0:T(4,128)S(1)} %get-tuple-element.144), kind=kOutput, calls=%fused_computation.16.clone.1 | convolution fusion | flops 545390592 | bytes 18096132 | tf_op jit(solution)/shard_map/while/body/eval_jaxpr/hqk,khd->qhd/dot_general | solution.py:35
  113.9 0.8 copy.26
  114.7 0.3 copy.33
  115.0 4.5 fusion.62
  119.5 0.0 reduce-scatter.2.cloned.1.call-update
  119.5 0.0 all-gather.2.cloned.1.call-start
  119.6 0.1 convert_reduce_fusion.1
  119.7 0.6 slice.26
  120.4 5.1 %collective-permute-start.1 = (f32[1]{0:T(128)}, f32[1]{0:T(128)}, u32[]{:S(2)}, u32[]{:S(2)}) collective-permute-start(f32[1]{0:T(128)} %slice.26), channel_id=1, source_target_pairs={{4,0},{8,4},{12,8},{16,12},{20,16},{24,20},{28,24},{32,28},{36,32}... | collective-permute-start | bytes 20 | tf_op jit(solution)/shard_map/ppermute | solution.py:15
  125.5 0.6 slice.34
  126.2 0.6 dynamic-slice
  127.4 0.7 compare_convert_fusion.2
  128.1 1.3 fusion.50
  129.5 77.1 %reduce-scatter.2.cloned.1.call-done = f32[2048,256]{1,0:T(8,128)} async-done(((f32[2048,1024]{1,0:T(8,128)}), f32[2048,256]{1,0:T(8,128)}) %reduce-scatter.2.cloned.1.call-update) | async-done | bytes 2097168 | tf_op jit(solution)/shard_map/reduce_scatter | solution.py:85
  206.6 2.9 fusion.33
  209.4 2.5 collective-permute-start
  212.0 2.3 collective-permute-done
  214.3 0.2 multiply_reduce_fusion.1
  214.5 6.6 %psum.14 = f32[32]{0:T(128)S(1)} all-reduce(f32[32]{0:T(128)S(1)} %multiply_reduce_fusion.1), channel_id=1, replica_groups=mesh['dp'=64,'mp'=4] {'mp'}, use_global_device_ids=true, to_apply=%region_9.10 | all-reduce | flops 32 | bytes 256 | tf_op jit(solution)/shard_map/psum | solution.py:96
  221.1 0.7 broadcast_multiply_fusion
  221.8 0.0 all-gather.2.cloned.1.call-update
  221.8 0.3 copy.28
  222.2 0.1 convert_dynamic-update-slice_fusion
  222.3 244.6 %all-reduce.2 = (f32[2048]{0:T(1024)S(1)}, f32[2048]{0:T(1024)S(1)}) all-reduce(f32[2048]{0:T(1024)S(1)} %convert_dynamic-update-slice_fusion, f32[2048]{0:T(1024)S(1)} %get-tuple-element.90), channel_id=1, replica_groups=mesh['dp'=64,'mp'=4] {'dp'}, use_global_device_ids=true, to_apply=%add.1 | all-reduce | flops 4096 | bytes 32768
  467.0 0.6 convert_reduce_fusion.2
  467.6 0.3 reduce-window.12
  467.9 0.1 slice.36
  468.0 0.1 slice_reduce_fusion
  468.1 0.1 broadcast_add_fusion
  468.2 14.9 %scatter_custom_fusion = s32[128]{0:T(128)S(1)} fusion(s32[2048]{0:T(1024)S(1)} %bitcast.61, s32[2048]{0:T(1024)S(1)} %broadcast.275, s32[]{:T(128)} %constant.118.clone.1), kind=kCustom, calls=%fused_computation.97 | custom fusion | flops 2048 | bytes 516 | tf_op jit(solution)/shard_map/scatter-add | solution.py:107
  483.1 0.1 copy.27
  483.2 0.2 select_n.123
  483.4 0.8 fusion.45
  484.2 1.2 gather_fusion
  485.3 0.7 compare_select_fusion.7
  486.0 0.3 fusion.38
  486.3 0.0 all-gather.2.cloned.1.call-done
  486.4 2.3 gather_fusion.1
  488.7 0.9 multiply_reduce_fusion
  489.6 6.9 %psum.15 = f32[1024]{0:T(1024)S(1)} all-reduce(f32[1024]{0:T(1024)S(1)} %get-tuple-element.96), channel_id=1, replica_groups=mesh['dp'=64,'mp'=4] {'mp'}, use_global_device_ids=true, to_apply=%region_17.18 | all-reduce | flops 1024 | bytes 8192 | tf_op jit(solution)/shard_map/psum | solution.py:118
  496.6 1.2 multiply_select_fusion.4
  497.7 2.5 copy.30
  (46 shorter events, 0.2 us)
Async XLA Ops:
  7.2 107.8 %copy-start = (bf16[256,1024]{1,0:T(8,128)(2,1)S(1)}, bf16[256,1024]{1,0:T(8,128)(2,1)}, u32[]{:S(2)}) copy-start(bf16[256,1024]{1,0:T(8,128)(2,1)} %param.18) | copy-start | bytes 1572868
  7.2 199.4 %reduce-scatter.2.cloned.1.call-start = ((), (), s32[]{:S(2)}) async-start(), calls=%async_computation.1 | async-start | bytes 10485760 | tf_op jit(solution)/shard_map/reduce_scatter | solution.py:85
  7.2 3.5 copy-start.1
  7.2 4.9 copy-start.5
  12.1 2.7 copy-start.7
  19.3 5.7 %copy-start.8 = (bf16[1024,256]{1,0:T(8,128)(2,1)S(1)}, bf16[1024,256]{1,0:T(8,128)(2,1)}, u32[]{:S(2)}) copy-start(bf16[1024,256]{1,0:T(8,128)(2,1)} %param.16) | copy-start | bytes 1572868
  25.0 4.6 copy-start.9
  29.6 4.6 copy-start.4
  29.6 4.6 copy-start.3
  119.5 6.7 %copy-start.11 = (u32[256]{0:T(256)S(1)}, u32[256]{0:T(256)}, u32[]{:S(2)}) copy-start(u32[256]{0:T(256)} %constant.138) | copy-start | bytes 3076
  119.5 102.4 %copy-start.2 = (f32[1024,256]{1,0:T(8,128)S(1)}, f32[1024,256]{1,0:T(8,128)}, u32[]{:S(2)}) copy-start(f32[1024,256]{1,0:T(8,128)} %param.19) | copy-start | bytes 3145732
  119.5 102.7 %copy-start.10 = (s32[32]{0:T(128)S(1)}, s32[32]{0:T(128)}, u32[]{:S(2)}) copy-start(s32[32]{0:T(128)} %param.21) | copy-start | bytes 388
  119.5 369.2 %copy-start.6 = (f32[1024]{0:T(1024)S(1)}, f32[1024]{0:T(1024)}, u32[]{:S(2)}) copy-start(f32[1024]{0:T(1024)} %param.20) | copy-start | bytes 12292
  119.5 366.8 %all-gather.2.cloned.1.call-start = ((), (), s32[]{:S(2)}) async-start(), calls=%async_computation.2 | async-start | bytes 2129920 | tf_op jit(solution)/shard_map/all_gather | solution.py:100
  120.4 7.7 %collective-permute-start.1 = (f32[1]{0:T(128)}, f32[1]{0:T(128)}, u32[]{:S(2)}, u32[]{:S(2)}) collective-permute-start(f32[1]{0:T(128)} %slice.26), channel_id=1, source_target_pairs={{4,0},{8,4},{12,8},{16,12},{20,16},{24,20},{28,24},{32,28},{36,32}... | collective-permute-start | bytes 20 | tf_op jit(solution)/shard_map/ppermute | solution.py:15
  209.4 4.9 collective-permute-start
Sparse Core Ops, SparseCore 0:
  119.6 86.8 reduce-scatter.1
  221.9 78.7 all-gather.1
where the time goes:
time: 514 us; the launch traced here: 507 us
  blocking collectives  258 us (50%)
  matrix products  98.6 us (19%)
  waiting for transfers between devices  79.5 us (15%)
  other arithmetic  31.8 us (6%)
  local copies, waits for them, and re-layouts  15.9 us (3%)
  between operations  15 us (3%)
  starting transfers between devices  7.74 us (2%)
    unnamed x1, blocking collectives  245 us
    reduce_scatter x1, waiting for transfers between devices, shards(): lax.psum_scatter(partial_out, 'mp', scatter_dimension=1, tiled=True)  77.1 us
    sub x4, matrix products, attend_block(): raised = jnp.exp(scores - top_score)  41.9 us
    dot_general x4, matrix products, attend_block(): jnp.einsum('hqk,khd->qhd', weights, values_all, preferred_element_type=jn...  34.9 us
    scatter-add x1, other arithmetic, shards(): jnp.nonzero(is_mine, size=kept_total, fill_value=0)[0].astype(jnp.int32)  14.9 us
    dot_general x3, matrix products, project(): jnp.dot(normed, weight, preferred_element_type=jnp.float32)  13.6 us
  transfers between devices with their start and end apart: 4, of which 2 were waited for; matrix products, arithmetic and copies ran while one was open for 5% of the time, Pallas kernels for 0%

commit v1 on v0

v1 whole, which is shorter than its diff:
```python
import functools
import math

import jax
import jax.numpy as jnp
from jax import lax
from jax.experimental import pallas as pl
from jax.experimental.pallas import tpu as pltpu
from jax.sharding import PartitionSpec as P

D = 1024
HEAD_DIM = 64
SEGS = 40
WIN = 128
LONG = 512
GROUP = 3
F32 = jnp.float32
BF16 = jnp.bfloat16
MESH = pl.DeviceIdType.MESH
NT = (((1,), (1,)), ((), ()))
NN = (((1,), (0,)), ((), ()))
EXP_SCALE = math.log2(math.e) / math.sqrt(HEAD_DIM)


def iota(shape, dim):
    return lax.broadcasted_iota(jnp.int32, shape, dim)


def halves(x):
    high = x.astype(BF16)
    return high, (x - high.astype(F32)).astype(BF16)


def to_column(row, n):
    full = jnp.broadcast_to(row, (n, n))
    return jnp.sum(jnp.where(iota((n, n), 0) == iota((n, n), 1), full, 0.0), axis=1, keepdims=True)


def to_row(column, n, width):
    full = jnp.broadcast_to(column, (n, width))
    return jnp.sum(jnp.where(iota((n, width), 0) == iota((n, width), 1), full, 0.0), axis=0, keepdims=True)


def pool_weights(p, inverse):
    n = inverse.shape[1]
    high = inverse.astype(BF16).astype(F32)
    low = inverse - high
    row = iota((16, n), 0)
    mine = (row < 4) & ((row & 1) == jnp.where(iota((16, n), 1) < n // 2, 0, 1))
    left = jnp.where(mine, jnp.where(row < 2, high, low), 0.0).astype(BF16)
    return lax.dot_general(left, p, NT, preferred_element_type=F32)


def weigh_values(sums, values):
    high, low = halves(sums)
    got = jnp.dot(high, values, preferred_element_type=F32) + jnp.dot(low, values, preferred_element_type=F32)
    row = iota((16, 128), 0)
    mine = (row & 1) == jnp.where(iota((16, 128), 1) < HEAD_DIM, 0, 1)
    return jnp.sum(jnp.where(mine, got, 0.0), axis=0, keepdims=True)


def rows_kernel(
    ids_ref, assigned_ref, tokens_ref, gain_ref, wq_ref, wk_ref, wv_ref, wo_ref,
    part_ref, carry_ref, cnt_ref, meta_ref, target_ref,
    q_s, k_s, v_s, tok_s, ctx_s, bound_v, bound_s, sc_s, p_s, sem,
):
    step = pl.program_id(0)
    last = pl.num_programs(0) - 1
    chunk = tokens_ref.shape[0]
    length = q_s.shape[0]
    width = wo_ref.shape[0]
    slots = 32
    r = lax.axis_index("dp")
    m = lax.axis_index("mp")

    @pl.when(step == 0)
    def _():
        local = ids_ref[...] - r * slots
        seg = iota((SEGS, length), 0)
        own = seg < slots
        carried = seg == slots
        starts = jnp.sum(jnp.where(own & (local < seg), 1.0, 0.0), axis=1, keepdims=True)
        ends = jnp.sum(
            jnp.where((own & (local <= seg)) | (carried & (local < 0)), 1.0, 0.0), axis=1, keepdims=True
        )
        lane = iota((SEGS, 128), 1)
        bound_v[...] = jnp.where(lane == 0, starts, ends).astype(jnp.int32)
        pltpu.make_async_copy(bound_v, bound_s, sem).start()
        counts = ends - starts
        picks = jnp.where((ends == float(length)) & (starts < float(length)), 1.0, 0.0)
        cnt_ref[...] = jnp.where(lane < 64, counts, picks)
        a_row = assigned_ref[...]
        used_row = to_row(counts[:slots], slots, slots) > 0
        d_row = jnp.where(used_row, ((a_row >> 10) - r) & 63, -1)
        d_col = to_column(d_row.astype(F32), slots)
        before = iota((slots, slots), 0) < iota((slots, slots), 1)
        same = d_col == d_row.astype(F32)
        rank_row = jnp.sum(jnp.where(before & same, 1.0, 0.0), axis=0, keepdims=True)
        spot = iota((64, slots), 0)
        local_row = ((a_row & 1023) + 1).astype(F32)
        here = spot == d_row
        first = jnp.sum(jnp.where(here & (rank_row == 0.0), local_row, 0.0), axis=1, keepdims=True)
        second = jnp.sum(jnp.where(here & (rank_row == 1.0), local_row, 0.0), axis=1, keepdims=True)
        place = (64 - iota((64, 128), 0)) & 63
        lane64 = iota((64, 128), 1)
        target_ref[...] = jnp.where(lane64 == place, first, 0.0) + jnp.where(lane64 == place + 64, second, 0.0)
        pick = (iota((slots, 128), 1) & 31) == iota((slots, 128), 0)
        rank_col = to_column(rank_row, slots)
        d_wide = jnp.sum(jnp.where(pick, d_col, 0.0), axis=0, keepdims=True)
        rank_wide = jnp.sum(jnp.where(pick, rank_col, 0.0), axis=0, keepdims=True)
        meta_ref[...] = jnp.where(iota((8, 128), 0) == 0, d_wide, rank_wide)

    sub = 128
    gain = gain_ref[...]
    low_half = (iota((sub, width), 1) & 127) < HEAD_DIM
    for j in range(chunk // sub):
        x = tokens_ref[j * sub : (j + 1) * sub, :].astype(F32)
        centered = x - jnp.mean(x, axis=1, keepdims=True)
        variance = jnp.mean(centered * centered, axis=1, keepdims=True)
        normed = (centered * lax.rsqrt(variance + 1e-05) * gain).astype(BF16)
        rows = pl.ds(pl.multiple_of(step * chunk + j * sub, sub), sub)
        q = jnp.dot(normed, wq_ref[...], preferred_element_type=F32)
        q_s[rows, 0:width] = jnp.where(low_half, q, 0.0).astype(BF16)
        q_s[rows, width : 2 * width] = jnp.where(low_half, 0.0, q).astype(BF16)
        k_s[rows, :] = jnp.dot(normed, wk_ref[...], preferred_element_type=F32).astype(BF16)
        v_s[rows, :] = jnp.dot(normed, wv_ref[...], preferred_element_type=F32).astype(BF16)

    local = ids_ref[:, pl.ds(pl.multiple_of(step * chunk, chunk), chunk)] - r * slots
    seg_of = jnp.where(local < 0, slots, local)
    member = jnp.where(iota((SEGS, chunk), 0) == seg_of, 1.0, 0.0).astype(BF16)
    columns = pl.ds(pl.multiple_of(m * width, width), width)
    got = jnp.dot(member, tokens_ref[:, columns], preferred_element_type=F32)
    tok_s[...] = jnp.where(step == 0, 0.0, tok_s[...]) + got

    @pl.when(step == last)
    def _():
        pltpu.make_async_copy(bound_v, bound_s, sem).wait()
        ctx_s[slots + 1 :] = jnp.zeros((SEGS - slots - 1, 1, width), F32)
        krow = iota((WIN, 1), 0)
        qlane = iota((1, 2 * WIN), 1) & (WIN - 1)

        def short(seg):
            start = bound_s[seg, 0]
            end = bound_s[seg, 1]
            base = pl.multiple_of(jnp.minimum((start // 16) * 16, length - WIN), 16)
            fits = end - base <= WIN
            stop = jnp.where(fits, end, start)
            bias = jnp.where((krow >= start - base) & (krow < stop - base), 0.0, -1e30)
            valid = (qlane >= start - base) & (qlane < stop - base)
            rows = pl.ds(base, WIN)
            for pair in range(width // 128):
                c0 = pair * 128
                q2 = jnp.concatenate(
                    [q_s[rows, c0 : c0 + 128], q_s[rows, width + c0 : width + c0 + 128]], axis=0
                )
                s = lax.dot_general(k_s[rows, c0 : c0 + 128], q2, NT, preferred_element_type=F32) + bias
                top = jnp.max(s, axis=0, keepdims=True)
                p = jnp.exp2((s - top) * EXP_SCALE)
                total = jnp.sum(p, axis=0, keepdims=True)
                inverse = jnp.where(valid, 1.0 / total, 0.0)
                sums = pool_weights(p.astype(BF16), inverse)
                ctx_s[seg, :, c0 : c0 + 128] = weigh_values(sums, v_s[rows, c0 : c0 + 128])

        @pl.loop(0, (slots + 1) // GROUP)
        def _(group):
            for j in range(GROUP):
                short(group * GROUP + j)

        lrow = iota((LONG, 1), 0)

        @pl.loop(0, slots + 1)
        def _(seg):
            start = bound_s[seg, 0]
            end = bound_s[seg, 1]
            base0 = jnp.minimum((start // 16) * 16, length - WIN)

            @pl.when(end - base0 > WIN)
            def _():
                base = (start // 16) * 16
                n_k = (end - base + LONG - 1) // LONG
                n_q = (end - base + WIN - 1) // WIN

                def k_rows(i):
                    at = pl.multiple_of(jnp.minimum(base + i * LONG, length - LONG), 16)
                    low = jnp.maximum(start, base + i * LONG) - at
                    bias = jnp.where((lrow >= low) & (lrow < end - at), 0.0, -1e30)
                    return pl.ds(at, LONG), pl.ds(pl.multiple_of(i * LONG, LONG), LONG), bias

                @pl.loop(0, n_q)
                def _(iq):
                    qs = base + iq * WIN
                    qat = pl.multiple_of(jnp.minimum(qs, length - WIN), 16)
                    valid = (qlane >= jnp.maximum(start, qs) - qat) & (qlane < end - qat)
                    qrows = pl.ds(qat, WIN)
                    for pair in range(width // 128):
                        c0 = pair * 128
                        q2 = jnp.concatenate(
                            [q_s[qrows, c0 : c0 + 128], q_s[qrows, width + c0 : width + c0 + 128]], axis=0
                        )

                        def scores(i, top):
                            krows, held, bias = k_rows(i)
                            s = lax.dot_general(
                                k_s[krows, c0 : c0 + 128], q2, NT, preferred_element_type=F32
                            ) + bias
                            sc_s[held, :] = s
                            return jnp.maximum(top, jnp.max(s, axis=0, keepdims=True))

                        top = lax.fori_loop(0, n_k, scores, jnp.full((1, 2 * WIN), -2e30, F32))

                        def raise_all(i, total):
                            krows, held, bias = k_rows(i)
                            p = jnp.exp2((sc_s[held, :] - top) * EXP_SCALE)
                            p_s[held, :] = p.astype(BF16)
                            return total + jnp.sum(p, axis=0, keepdims=True)

                        total = lax.fori_loop(0, n_k, raise_all, jnp.zeros((1, 2 * WIN), F32))
                        inverse = jnp.where(valid, 1.0 / total, 0.0)

                        def weigh(i, acc):
                            krows, held, bias = k_rows(i)
                            sums = pool_weights(p_s[held, :], inverse)
                            return acc + weigh_values(sums, v_s[krows, c0 : c0 + 128])

                        acc = lax.fori_loop(0, n_k, weigh, jnp.zeros((1, 128), F32))
                        ctx_s[seg, :, c0 : c0 + 128] += acc

        high, low = halves(ctx_s[...].reshape(SEGS, width))
        out = jnp.dot(high, wo_ref[...], preferred_element_type=F32) + jnp.dot(
            low, wo_ref[...], preferred_element_type=F32
        )
        carried_count = jnp.broadcast_to(bound_s[slots, 1].astype(F32), (8, width))
        row8 = iota((8, width), 0)
        for mm in range(part_ref.shape[0]):
            block = out[:, mm * width : (mm + 1) * width] + jnp.where(m == mm, tok_s[...], 0.0)
            part_ref[mm] = block[:slots]
            carry_ref[mm] = jnp.where(row8 == 1, carried_count, block[slots : slots + 8])


def exchange_kernel(
    dp, mp, part_ref, carry_ref, cnt_ref, meta_ref, target_ref, mass_ref, cent_ref,
    docs_ref, rows_ref, tgt_ref,
    got_part, got_carry, tsend, tgot, ss_send, ss_got, csend, cgot, n_send, n_got, cent_v,
    part_sems, carry_sems, t_sems, ss_sems, c_sems, n_sems, cent_sem,
):
    r = lax.axis_index("dp")
    m = lax.axis_index("mp")
    slots = 32
    cents = cent_v.shape[0]
    width = cent_v.shape[1]
    load = pltpu.make_async_copy(cent_ref, cent_v, cent_sem)
    load.start()

    barrier = pltpu.get_barrier_semaphore()
    nxt = lax.rem(r + 1, dp)
    prv = lax.rem(r + dp - 1, dp)
    for dm in range(1, mp):
        mm = lax.rem(m + dm, mp)
        pl.semaphore_signal(barrier, inc=1, device_id=(r, mm), device_id_type=MESH)
        pl.semaphore_signal(barrier, inc=1, device_id=(nxt, mm), device_id_type=MESH)

    @pl.loop(1, dp)
    def _(d):
        pl.semaphore_signal(barrier, inc=1, device_id=(lax.rem(r + d, dp), m), device_id_type=MESH)

    tsend[...] = target_ref[...].reshape(dp, 1, 128)
    tgot[0] = tsend[0]
    pl.semaphore_wait(barrier, dp - 1 + 2 * (mp - 1))

    def to_peer(src, dst, sems, dm):
        mm = lax.rem(m + dm, mp)
        return pltpu.make_async_remote_copy(
            src_ref=src, dst_ref=dst, send_sem=sems.at[0], recv_sem=sems.at[1],
            device_id=(r, mm), device_id_type=MESH,
        )

    for dm in range(1, mp):
        to_peer(part_ref.at[lax.rem(m + dm, mp)], got_part.at[mp - 1 - dm], part_sems, dm).start()
    for mm in range(mp):
        pltpu.make_async_remote_copy(
            src_ref=carry_ref.at[mm], dst_ref=got_carry.at[m], send_sem=carry_sems.at[0],
            recv_sem=carry_sems.at[1], device_id=(prv, mm), device_id_type=MESH,
        ).start()

    @pl.loop(1, dp)
    def _(d):
        pltpu.make_async_remote_copy(
            src_ref=tsend.at[d], dst_ref=tgot.at[dp - d], send_sem=t_sems.at[0], recv_sem=t_sems.at[1],
            device_id=(lax.rem(r + d, dp), m), device_id_type=MESH,
        ).start()

    d_wide = meta_ref[0:1, :]
    rank_wide = meta_ref[1:2, :]
    row = iota((8 * dp, 128), 0)
    col = iota((8 * dp, 128), 1)
    j = row & 7
    pick = (
        ((row >> 3).astype(F32) == d_wide)
        & ((j >> 1).astype(F32) == rank_wide)
        & ((j & 1) == ((col >> 5) & 1))
    )
    pick = jnp.where(pick, 1.0, 0.0).astype(BF16)

    def wait_all(buffer, sem):
        pltpu.make_async_copy(buffer, buffer, sem).wait()

    wait_all(got_part, part_sems.at[1])
    wait_all(got_carry, carry_sems.at[1])
    sums = part_ref[m]
    for i in range(mp - 1):
        sums = sums + got_part[i]
    carry = got_carry[0]
    for i in range(1, mp):
        carry = carry + got_carry[i]
    count_in = got_carry[0][1:2, :]
    counts = cnt_ref[0:slots, 0:1]
    picks = cnt_ref[0:slots, 64:65]
    sums = sums + picks * carry[0:1, :]
    totals = counts + picks * count_in
    averages = sums / jnp.maximum(totals, 1.0)
    squares = jnp.sum(averages * averages, axis=1, keepdims=True)
    square_row = to_row(squares, slots, 128)
    ss_send[...] = jnp.broadcast_to(square_row, (8, 128))
    for dm in range(1, mp):
        to_peer(ss_send, ss_got.at[mp - 1 - dm], ss_sems, dm).start()
    wait_all(ss_got, ss_sems.at[1])
    for i in range(mp - 1):
        square_row = square_row + ss_got[i][0:1, :]
    eye = iota((slots, 128), 0) == iota((slots, 128), 1)
    squares = jnp.sum(jnp.where(eye, square_row, 0.0), axis=1, keepdims=True)
    vectors = averages * lax.rsqrt(squares * (1.0 / D) + 1e-06)
    docs_ref[...] = vectors

    high, low = halves(vectors)
    high, low = high.astype(F32), low.astype(F32)
    stacked = jnp.concatenate([high[:, :128], high[:, 128:], low[:, :128], low[:, 128:]], axis=0).astype(BF16)
    outgoing = jnp.dot(pick, stacked, preferred_element_type=F32).reshape(dp, 8, 128)
    csend[...] = outgoing[:, :4, :]
    cgot[0] = csend[0]

    @pl.loop(1, dp)
    def _(d):
        pltpu.make_async_remote_copy(
            src_ref=csend.at[d], dst_ref=cgot.at[dp - d], send_sem=c_sems.at[0], recv_sem=c_sems.at[1],
            device_id=(lax.rem(r + d, dp), m), device_id_type=MESH,
        ).start()

    rest = pl.ds(1, dp - 1)
    wait_all(tgot.at[rest], t_sems.at[1])
    tgt_row = jnp.sum(tgot[...], axis=0)
    tgt_col = to_column(tgt_row, 128)
    tgt_ref[...] = jnp.broadcast_to(tgt_row, (8, 128))
    load.wait()
    hits = jnp.where(iota((128, cents), 1).astype(F32) == tgt_col - 1.0, 1.0, 0.0)
    mass = jnp.sum(hits * mass_ref[...], axis=1, keepdims=True)
    hits = hits.astype(BF16)
    cent_high, cent_low = halves(cent_v[...])
    picked = jnp.dot(hits, cent_high, preferred_element_type=F32) + jnp.dot(
        hits, cent_low, preferred_element_type=F32
    )
    start = mass * picked
    together = jnp.where((tgt_col == tgt_row) & (tgt_row > 0.0), 1.0, 0.0).astype(BF16)

    wait_all(cgot.at[rest], c_sems.at[1])
    arrived = jnp.concatenate(
        [
            jnp.concatenate([cgot[:, 2 * k, :], cgot[:, 2 * k + 1, :]], axis=1)
            for k in range(2)
        ],
        axis=0,
    )
    high, low = halves(arrived)
    blended = start + (
        jnp.dot(together, high, preferred_element_type=F32) + jnp.dot(together, low, preferred_element_type=F32)
    )
    norm_row = to_row(jnp.sum(blended * blended, axis=1, keepdims=True), 128, 128)
    n_send[...] = jnp.broadcast_to(norm_row, (8, 128))
    for dm in range(1, mp):
        to_peer(n_send, n_got.at[mp - 1 - dm], n_sems, dm).start()
    wait_all(n_got, n_sems.at[1])
    for i in range(mp - 1):
        norm_row = norm_row + n_got[i][0:1, :]
    norms = to_column(norm_row, 128)
    rows_ref[...] = blended * lax.rsqrt(norms * (1.0 / D) + 1e-06)

    wait_all(got_part, part_sems.at[0])
    wait_all(got_carry, carry_sems.at[0])
    wait_all(tsend.at[rest], t_sems.at[0])
    wait_all(ss_got, ss_sems.at[0])
    wait_all(csend.at[rest], c_sems.at[0])
    wait_all(n_got, n_sems.at[0])


def write_kernel(docs_ref, rows_ref, tgt_ref, cent_ref, docs_out, out_ref):
    step = pl.program_id(0)
    block = cent_ref.shape[0]

    @pl.when(step == 0)
    def _():
        docs_out[...] = docs_ref[...]

    tgt_row = tgt_ref[0:1, :]
    tgt_col = to_column(tgt_row, 128)
    earlier = iota((128, 128), 0) < iota((128, 128), 1)
    repeats = jnp.sum(jnp.where(earlier & (tgt_col == tgt_row), 1.0, 0.0), axis=0, keepdims=True)
    wanted = jnp.where(repeats == 0.0, tgt_row - 1.0, -1.0)
    index = (iota((block, 128), 0) + step * block).astype(F32)
    hits = jnp.where(index == wanted, 1.0, 0.0)
    touched = jnp.sum(hits, axis=1, keepdims=True) > 0.0
    hits = hits.astype(BF16)
    high, low = halves(rows_ref[...])
    new = jnp.dot(hits, high, preferred_element_type=F32) + jnp.dot(hits, low, preferred_element_type=F32)
    out_ref[...] = jnp.where(touched, new, cent_ref[...])


def shards(
    tokens, doc_ids, ln_gain, w_query, w_key, w_value, w_out, centroids, cluster_mass, assigned
):
    length = tokens.shape[0]
    width = w_out.shape[0]
    slots = assigned.shape[0]
    cents = centroids.shape[0]
    dp, mp = lax.axis_size("dp"), lax.axis_size("mp")
    chunk = 256

    def whole(*shape):
        return pl.BlockSpec(shape, lambda i: (0,) * len(shape))

    def shape(*dims):
        return jax.ShapeDtypeStruct(dims, F32)

    part, carry, cnt, meta, target = pl.pallas_call(
        rows_kernel,
        grid=(length // chunk,),
        in_specs=[
            whole(1, length), whole(1, slots), pl.BlockSpec((chunk, D), lambda i: (i, 0)), whole(1, D),
            whole(D, width), whole(D, width), whole(D, width), whole(width, D),
        ],
        out_specs=[whole(mp, slots, width), whole(mp, 8, width), whole(SEGS, 128), whole(8, 128), whole(dp, 128)],
        out_shape=[shape(mp, slots, width), shape(mp, 8, width), shape(SEGS, 128), shape(8, 128), shape(dp, 128)],
        scratch_shapes=[
            pltpu.VMEM((length, 2 * width), BF16),
            pltpu.VMEM((length, width), BF16),
            pltpu.VMEM((length, width), BF16),
            pltpu.VMEM((SEGS, width), F32),
            pltpu.VMEM((SEGS, 1, width), F32),
            pltpu.VMEM((SEGS, 128), jnp.int32),
            pltpu.SMEM((SEGS, 128), jnp.int32),
            pltpu.VMEM((length + LONG, 2 * WIN), F32),
            pltpu.VMEM((length + LONG, 2 * WIN), BF16),
            pltpu.SemaphoreType.DMA,
        ],
        compiler_params=pltpu.CompilerParams(vmem_limit_bytes=48 << 20),
        name="rows",
    )(
        doc_ids.reshape(1, length), assigned.reshape(1, slots), tokens, ln_gain.reshape(1, D),
        w_query, w_key, w_value, w_out,
    )

    vmem = pl.BlockSpec(memory_space=pltpu.VMEM)
    pair = pltpu.SemaphoreType.DMA((2,))
    docs, rows, tgt = pl.pallas_call(
        functools.partial(exchange_kernel, dp, mp),
        in_specs=[vmem] * 6 + [pl.BlockSpec(memory_space=pl.ANY)],
        out_specs=[vmem] * 3,
        out_shape=[shape(slots, width), shape(128, width), shape(8, 128)],
        scratch_shapes=[
            pltpu.VMEM((mp - 1, slots, width), F32),
            pltpu.VMEM((mp, 8, width), F32),
            pltpu.VMEM((dp, 1, 128), F32),
            pltpu.VMEM((dp, 1, 128), F32),
            pltpu.VMEM((8, 128), F32),
            pltpu.VMEM((mp - 1, 8, 128), F32),
            pltpu.VMEM((dp, 4, 128), F32),
            pltpu.VMEM((dp, 4, 128), F32),
            pltpu.VMEM((8, 128), F32),
            pltpu.VMEM((mp - 1, 8, 128), F32),
            pltpu.VMEM((cents, width), F32),
            pair, pair, pair, pair, pair, pair,
            pltpu.SemaphoreType.DMA,
        ],
        compiler_params=pltpu.CompilerParams(
            collective_id=0, has_side_effects=True, vmem_limit_bytes=32 << 20
        ),
        name="exchange",
    )(part, carry, cnt, meta, target, cluster_mass.reshape(1, cents), centroids)

    block = 256
    docs_out, updated = pl.pallas_call(
        write_kernel,
        grid=(cents // block,),
        in_specs=[whole(slots, width), whole(128, width), whole(8, 128), pl.BlockSpec((block, width), lambda i: (i, 0))],
        out_specs=[whole(slots, width), pl.BlockSpec((block, width), lambda i: (i, 0))],
        out_shape=[shape(slots, width), shape(cents, width)],
        name="write",
    )(docs, rows, tgt, centroids)
    return (docs_out, updated)


def solution(mesh):
    placed = (
        P("dp", None),
        P("dp"),
        P(),
        P(None, "mp"),
        P(None, "mp"),
        P(None, "mp"),
        P("mp", None),
        P("dp", "mp"),
        P("dp"),
        P("dp"),
    )
    return jax.shard_map(
        shards,
        mesh=mesh,
        in_specs=placed,
        out_specs=(P("dp", "mp"), P("dp", "mp")),
        check_vma=False,
    )
```

time: 514 us -> 70.3 us (0.14); the launches traced: 507 us -> 69.8 us
  blocking collectives: 258 us -> 0 us
  matrix products: 98.6 us -> 0 us
  waiting for transfers between devices: 79.5 us -> 0 us
  Pallas kernels: 0 us -> 61 us
  other arithmetic: 31.8 us -> 0 us
  between operations: 15 us -> 0.7 us
  local copies, waits for them, and re-layouts: 15.9 us -> 8.12 us
  starting transfers between devices: 7.74 us -> 0 us
    unnamed x1 -> x0, blocking collectives: 245 us -> none
    reduce_scatter x1 -> x0, waiting for transfers between devices: 77.1 us -> none  [shards(): lax.psum_scatter(partial_out, 'mp', scatter_dimension=1, tiled=True)]
    pallas_call x0 -> x3, Pallas kernels: none -> 61 us  [the longest x1 32.1 us: shards(): pl.pallas_call(functools.partial(exchange_kernel, dp, mp), in_specs=[vmem...]
    dot_general x10 -> x0, matrix products: 56.7 us -> none  [the longest x4 34.9 us: attend_block(): jnp.einsum('hqk,khd->qhd', weights, values_all, preferred_element_type=jn...]
    sub x4 -> x0, matrix products: 41.9 us -> none  [attend_block(): raised = jnp.exp(scores - top_score)]
    scatter-add x1 -> x0, other arithmetic: 14.9 us -> none  [shards(): jnp.nonzero(is_mine, size=kept_total, fill_value=0)[0].astype(jnp.int32)]
    psum x2 -> x0, blocking collectives: 13.5 us -> none  [the longest x1 6.94 us: shards(): norm_terms = lax.psum(jnp.sum(blended * blended, axis=1), 'mp')]
    ppermute x2 -> x0, starting transfers between devices: 7.66 us -> none  [shifted(): return lax.ppermute(x, axis, pairs)]
  transfers between devices with their start and end apart: 4 -> 0, of which waited for: 2 -> 0; matrix products, arithmetic and copies ran while one was open for 5% -> 0% of each run, Pallas kernels for 0% -> 0%
where the time goes in v1:
time: 70.3 us; the launch traced here: 69.8 us
  Pallas kernels  61 us (87%)
  local copies, waits for them, and re-layouts  8.12 us (12%)
    pallas_call x1, Pallas kernels, shards(): pl.pallas_call(functools.partial(exchange_kernel, dp, mp), in_specs=[vmem...  32.1 us
    pallas_call x1, Pallas kernels, shards(): pl.pallas_call(rows_kernel, grid=(length // chunk,), in_specs=[whole(1, l...  24.9 us
    unnamed x24, local copies, waits for them, and re-layouts  8.12 us
    pallas_call x1, Pallas kernels, shards(): pl.pallas_call(write_kernel, grid=(cents // block,), in_specs=[whole(slot...  3.98 us

profile of v1, /device:TPU:1, one launch (start us, length us, event | category | flops | bytes accessed | tf_op | source)
XLA Modules:
  0.0 69.8 jit_solution(12907738310580173513)
XLA Ops:
  0.6 0.0 copy-start
  0.6 0.0 copy-start.1
  0.7 1.1 %copy-done.1 = bf16[1024,256]{1,0:T(8,128)(2,1)S(1)} copy-done((bf16[1024,256]{1,0:T(8,128)(2,1)S(1)}, bf16[1024,256]{1,0:T(8,128)(2,1)}, u32[]{:S(2)}) %copy-start.1) | copy-done | bytes 524312
  1.8 0.0 copy-start.2
  1.8 1.0 %copy-done.2 = bf16[1024,256]{1,0:T(8,128)(2,1)S(1)} copy-done((bf16[1024,256]{1,0:T(8,128)(2,1)S(1)}, bf16[1024,256]{1,0:T(8,128)(2,1)}, u32[]{:S(2)}) %copy-start.2) | copy-done | bytes 524312
  2.8 0.0 copy-start.3
  2.8 1.0 %copy-done.3 = bf16[1024,256]{1,0:T(8,128)(2,1)S(1)} copy-done((bf16[1024,256]{1,0:T(8,128)(2,1)S(1)}, bf16[1024,256]{1,0:T(8,128)(2,1)}, u32[]{:S(2)}) %copy-start.3) | copy-done | bytes 524312
  3.9 0.0 copy-start.4
  3.9 1.0 %copy-done.4 = bf16[256,1024]{1,0:T(8,128)(2,1)S(1)} copy-done((bf16[256,1024]{1,0:T(8,128)(2,1)S(1)}, bf16[256,1024]{1,0:T(8,128)(2,1)}, u32[]{:S(2)}) %copy-start.4) | copy-done | bytes 524312
  4.9 0.0 copy-start.7
  4.9 0.7 copy-done.7
  5.6 0.0 copy-start.10
  5.6 0.7 copy-done.10
  6.3 0.0 copy-start.11
  6.3 0.7 copy-done.11
  6.9 0.0 copy-start.8
  6.9 24.9 %rows.1 = (f32[4,32,256]{2,1,0:T(8,128)S(1)}, f32[4,8,256]{2,1,0:T(8,128)S(1)}, f32[40,128]{1,0:T(8,128)S(1)}, f32[8,128]{1,0:T(8,128)S(1)}, f32[64,128]{1,0:T(8,128)S(1)}) custom-call(s32[1,2048]{1,0:T(1,128)S(1)} %bitcast.4, s32[1,32]{1,0:T(1,128)S(1)} %bitcast.7, bf16[2048,1024]{1,0:T(8,128)(2,1)} %tokens_ref.1, f32[1,1024]{1,0:T(1,128)S(1)} %bitcast.6, ...), custom_call_target="tpu_custom_call" | custom-call | tf_op jit(solution)/shard_map/rows/pallas_call | solution.py:432
  31.9 0.0 copy-done
  31.9 0.0 copy-done.8
  31.9 32.1 %exchange.1 = (f32[32,256]{1,0:T(8,128)S(1)}, f32[128,256]{1,0:T(8,128)S(1)}, f32[8,128]{1,0:T(8,128)S(1)}) custom-call(f32[4,32,256]{2,1,0:T(8,128)S(1)} %get-tuple-element.10.part_ref, f32[4,8,256]{2,1,0:T(8,128)S(1)} %get-tuple-element.11.carry_ref, f32[40,128]{1,0:T(8,128)S(1)} %get-tuple-element.12.cnt_ref, f32[8,128]{1,0:T(8,128)S(1)} %get-tuple-element.13.meta_ref, ...), custom_call_target="tpu_custom_call" | custom-call | tf_op jit(solution)/shard_map/exchange/pallas_call | solution.py:462
  64.0 0.0 copy-start.5
  64.0 0.6 copy-done.5
  64.7 0.0 copy-start.6
  64.7 0.6 copy-done.6
  65.3 0.0 copy-start.9
  65.3 0.6 copy-done.9
  65.9 4.0 %write.1 = (f32[32,256]{1,0:T(8,128)}, f32[1024,256]{1,0:T(8,128)}) custom-call(f32[32,256]{1,0:T(8,128)} %copy-done.6, f32[128,256]{1,0:T(8,128)} %copy-done.5, f32[8,128]{1,0:T(8,128)} %copy-done.9, f32[1024,256]{1,0:T(8,128)} %cent_ref.3), custom_call_target="tpu_custom_call" | custom-call | tf_op jit(solution)/shard_map/write/pallas_call | solution.py:489
Async XLA Ops:
  0.6 31.2 %copy-start = (f32[1024,256]{1,0:T(8,128)S(1)}, f32[1024,256]{1,0:T(8,128)}, u32[]{:S(2)}) copy-start(f32[1024,256]{1,0:T(8,128)} %cent_ref.3) | copy-start | bytes 3145732
  0.6 1.1 %copy-start.1 = (bf16[1024,256]{1,0:T(8,128)(2,1)S(1)}, bf16[1024,256]{1,0:T(8,128)(2,1)}, u32[]{:S(2)}) copy-start(bf16[1024,256]{1,0:T(8,128)(2,1)} %wq_ref.1) | copy-start | bytes 1572868
  1.8 1.0 %copy-start.2 = (bf16[1024,256]{1,0:T(8,128)(2,1)S(1)}, bf16[1024,256]{1,0:T(8,128)(2,1)}, u32[]{:S(2)}) copy-start(bf16[1024,256]{1,0:T(8,128)(2,1)} %wk_ref.1) | copy-start | bytes 1572868
  2.8 1.0 %copy-start.3 = (bf16[1024,256]{1,0:T(8,128)(2,1)S(1)}, bf16[1024,256]{1,0:T(8,128)(2,1)}, u32[]{:S(2)}) copy-start(bf16[1024,256]{1,0:T(8,128)(2,1)} %wv_ref.1) | copy-start | bytes 1572868
  3.9 1.0 %copy-start.4 = (bf16[256,1024]{1,0:T(8,128)(2,1)S(1)}, bf16[256,1024]{1,0:T(8,128)(2,1)}, u32[]{:S(2)}) copy-start(bf16[256,1024]{1,0:T(8,128)(2,1)} %wo_ref.1) | copy-start | bytes 1572868
  4.9 0.7 copy-start.7
  5.6 0.7 copy-start.10
  6.3 0.7 copy-start.11
  6.9 24.9 %copy-start.8 = (f32[1024]{0:T(1024)S(1)}, f32[1024]{0:T(1024)}, u32[]{:S(2)}) copy-start(f32[1024]{0:T(1024)} %param.18) | copy-start | bytes 12292
  64.0 0.7 copy-start.5
  64.7 0.6 copy-start.6
  65.3 0.6 copy-start.9

commit v2 on v1

v2 whole, which is shorter than its diff:
```python
import functools
import math

import jax
import jax.numpy as jnp
from jax import lax
from jax.experimental import pallas as pl
from jax.experimental.pallas import tpu as pltpu
from jax.sharding import PartitionSpec as P

D = 1024
HEAD_DIM = 64
SEGS = 40
WIN = 128
LONG = 512
GROUP = 11
F32 = jnp.float32
BF16 = jnp.bfloat16
MESH = pl.DeviceIdType.MESH
NT = (((1,), (1,)), ((), ()))
NN = (((1,), (0,)), ((), ()))
EXP_SCALE = math.log2(math.e) / math.sqrt(HEAD_DIM)


def iota(shape, dim):
    return lax.broadcasted_iota(jnp.int32, shape, dim)


def halves(x):
    high = x.astype(BF16)
    return high, (x - high.astype(F32)).astype(BF16)


def to_column(row, n):
    full = jnp.broadcast_to(row, (n, n))
    return jnp.sum(jnp.where(iota((n, n), 0) == iota((n, n), 1), full, 0.0), axis=1, keepdims=True)


def to_row(column, n, width):
    full = jnp.broadcast_to(column, (n, width))
    return jnp.sum(jnp.where(iota((n, width), 0) == iota((n, width), 1), full, 0.0), axis=0, keepdims=True)


def block_sums(k, q2, v, bias, valid):
    s = lax.dot_general(k, q2, NT, preferred_element_type=F32) + bias
    top = jnp.max(s, axis=0, keepdims=True)
    p = jnp.exp2((s - top) * EXP_SCALE)
    total = jnp.sum(p, axis=0, keepdims=True)
    weighted = p * jnp.where(valid, 1.0 / total, 0.0)
    first = jnp.sum(weighted[:, :WIN], axis=1, keepdims=True)
    second = jnp.sum(weighted[:, WIN:], axis=1, keepdims=True)
    sums = jnp.where(iota((1, 128), 1) < HEAD_DIM, first, second)
    return jnp.sum(sums * v.astype(F32), axis=0, keepdims=True)


def rows_kernel(
    ids_hbm, assigned_hbm, gain_hbm, tokens_hbm, wq_hbm, wk_hbm, wv_hbm,
    q_ref, k_ref, v_ref, ctx_ref, tok_ref, bound_ref, meta_ref, target_ref,
    ids_v, assigned_v, gain_v, tokens_v, w_v, normed_v, bound_s, sc_s, sems, token_sems, bound_sem,
):
    length = q_ref.shape[0] * 16
    width = k_ref.shape[2]
    slots = 32
    parts = token_sems.shape[0]
    piece = length // parts
    r = lax.axis_index("dp")
    m = lax.axis_index("mp")

    small = [
        pltpu.make_async_copy(src, dst, sems.at[i])
        for i, (src, dst) in enumerate(((ids_hbm, ids_v), (assigned_hbm, assigned_v), (gain_hbm, gain_v)))
    ]
    weights = [
        pltpu.make_async_copy(src, w_v.at[:, i * width : (i + 1) * width], sems.at[3 + i])
        for i, src in enumerate((wq_hbm, wk_hbm, wv_hbm))
    ]
    pieces = [
        pltpu.make_async_copy(
            tokens_hbm.at[pl.ds(i * piece, piece)], tokens_v.at[pl.ds(i * piece, piece)], token_sems.at[i]
        )
        for i in range(parts)
    ]
    for copy in small + pieces[:2] + weights + pieces[2:]:
        copy.start()
    for copy in small:
        copy.wait()

    local = ids_v[...] - r * slots
    seg = iota((SEGS, length), 0)
    own = seg < slots
    carried = seg == slots
    starts = jnp.sum(jnp.where(own & (local < seg), 1.0, 0.0), axis=1, keepdims=True)
    ends = jnp.sum(jnp.where((own & (local <= seg)) | (carried & (local < 0)), 1.0, 0.0), axis=1, keepdims=True)
    lane = iota((SEGS, 128), 1)
    at_row = jnp.minimum(jnp.floor(starts * (1.0 / 16.0)) * 16.0, float(length - WIN))
    fits = ends - at_row <= float(WIN)
    bound_ref[...] = jnp.where(
        lane == 0,
        starts,
        jnp.where(lane == 1, ends, jnp.where(lane == 2, at_row * (1.0 / 16.0), jnp.where(lane == 3, starts - at_row, jnp.where(fits, ends, starts) - at_row))),
    ).astype(jnp.int32)
    to_scalars = pltpu.make_async_copy(bound_ref, bound_s, bound_sem)
    to_scalars.start()
    counts = ends - starts
    picks = jnp.where((ends == float(length)) & (starts < float(length)), 1.0, 0.0)
    meta_ref[8:, :] = jnp.where(lane < 64, counts, picks)
    a_row = assigned_v[...]
    used_row = to_row(counts[:slots], slots, slots) > 0
    d_row = jnp.where(used_row, ((a_row >> 10) - r) & 63, -1)
    d_col = to_column(d_row.astype(F32), slots)
    before = iota((slots, slots), 0) < iota((slots, slots), 1)
    same = d_col == d_row.astype(F32)
    rank_row = jnp.sum(jnp.where(before & same, 1.0, 0.0), axis=0, keepdims=True)
    spot = iota((64, slots), 0)
    local_row = ((a_row & 1023) + 1).astype(F32)
    here = spot == d_row
    first = jnp.sum(jnp.where(here & (rank_row == 0.0), local_row, 0.0), axis=1, keepdims=True)
    second = jnp.sum(jnp.where(here & (rank_row == 1.0), local_row, 0.0), axis=1, keepdims=True)
    place = (64 - iota((64, 128), 0)) & 63
    lane64 = iota((64, 128), 1)
    target_ref[...] = jnp.where(lane64 == place, first, 0.0) + jnp.where(lane64 == place + 64, second, 0.0)
    pick = (iota((slots, 128), 1) & 31) == iota((slots, 128), 0)
    rank_col = to_column(rank_row, slots)
    d_wide = jnp.sum(jnp.where(pick, d_col, 0.0), axis=0, keepdims=True)
    rank_wide = jnp.sum(jnp.where(pick, rank_col, 0.0), axis=0, keepdims=True)
    meta_ref[:8, :] = jnp.where(iota((8, 128), 0) == 0, d_wide, rank_wide)
    ctx_ref[...] = jnp.zeros_like(ctx_ref)

    half = length // 2
    gain = gain_v[...]
    low_half = (iota((half, width), 1) & 127) < HEAD_DIM

    def norm(i):
        rows = slice(i * piece, (i + 1) * piece)
        x = tokens_v[rows, :].astype(F32)
        centered = x - jnp.mean(x, axis=1, keepdims=True)
        variance = jnp.mean(centered * centered, axis=1, keepdims=True)
        normed_v[rows, :] = (centered * lax.rsqrt(variance + 1e-05) * gain).astype(BF16)

    def project(i):
        rows = slice(i * half, (i + 1) * half)
        blocks = slice(i * half // 16, (i + 1) * half // 16)
        out = jnp.dot(normed_v[rows, :], w_v[...], preferred_element_type=F32)
        q = out[:, :width]
        q_ref[blocks, :, 0:width] = jnp.where(low_half, q, 0.0).astype(BF16).reshape(half // 16, 16, width)
        q_ref[blocks, :, width : 2 * width] = jnp.where(low_half, 0.0, q).astype(BF16).reshape(half // 16, 16, width)
        k_ref[blocks] = out[:, width : 2 * width].astype(BF16).reshape(half // 16, 16, width)
        v_ref[blocks] = out[:, 2 * width :].astype(BF16).reshape(half // 16, 16, width)

    for i in range(parts // 2):
        pieces[i].wait()
        norm(i)
    for copy in weights + pieces[parts // 2 :]:
        copy.wait()
    project(0)
    for i in range(parts // 2, parts):
        norm(i)
    project(1)

    seg_of = jnp.where(local < 0, slots, local)
    member = jnp.where(seg == seg_of, 1.0, 0.0).astype(BF16)
    columns = pl.ds(pl.multiple_of(m * width, width), width)
    tok_ref[...] = jnp.dot(member, tokens_v[:, columns], preferred_element_type=F32)

    to_scalars.wait()
    qlane = iota((1, 2 * WIN), 1) & (WIN - 1)

    def taken(ref, at, n, c0):
        return ref[pl.ds(at // 16, n // 16), :, c0 : c0 + 128].reshape(n, 128)

    def queries(at, c0):
        return jnp.concatenate([taken(q_ref, at, WIN, c0), taken(q_ref, at, WIN, width + c0)], axis=0)

    def long(seg, start, end, reach):
        first = (start // 16) * 16
        base = pl.multiple_of(jnp.minimum(first, length - reach), 16)
        row = iota((reach, 1), 0)
        bias = jnp.where((row >= start - base) & (row < end - base), 0.0, -1e30)

        @pl.loop(0, (end - first + WIN - 1) // WIN)
        def _(i):
            qs = first + i * WIN
            at = pl.multiple_of(jnp.minimum(qs, length - WIN), 16)
            valid = (qlane >= jnp.maximum(start, qs) - at) & (qlane < end - at)
            for pair in range(width // 128):
                c0 = pair * 128
                ctx_ref[seg, :, c0 : c0 + 128] += block_sums(
                    taken(k_ref, base, reach, c0), queries(at, c0), taken(v_ref, base, reach, c0), bias, valid
                )

    def longest(seg, start, end):
        first = (start // 16) * 16
        n_k = (end - first + LONG - 1) // LONG
        row = iota((LONG, 1), 0)

        def k_rows(i):
            at = pl.multiple_of(jnp.minimum(first + i * LONG, length - LONG), 16)
            low = jnp.maximum(start, first + i * LONG) - at
            bias = jnp.where((row >= low) & (row < end - at), 0.0, -1e30)
            return at, pl.ds(pl.multiple_of(i * LONG, LONG), LONG), bias

        @pl.loop(0, (end - first + WIN - 1) // WIN)
        def _(iq):
            qs = first + iq * WIN
            qat = pl.multiple_of(jnp.minimum(qs, length - WIN), 16)
            valid = (qlane >= jnp.maximum(start, qs) - qat) & (qlane < end - qat)
            for pair in range(width // 128):
                c0 = pair * 128
                q2 = queries(qat, c0)

                def scores(i, top):
                    krows, held, bias = k_rows(i)
                    s = lax.dot_general(taken(k_ref, krows, LONG, c0), q2, NT, preferred_element_type=F32) + bias
                    sc_s[held, :] = s
                    return jnp.maximum(top, jnp.max(s, axis=0, keepdims=True))

                top = lax.fori_loop(0, n_k, scores, jnp.full((1, 2 * WIN), -2e30, F32))

                def raise_all(i, total):
                    krows, held, bias = k_rows(i)
                    p = jnp.exp2((sc_s[held, :] - top) * EXP_SCALE)
                    sc_s[held, :] = p
                    return total + jnp.sum(p, axis=0, keepdims=True)

                total = lax.fori_loop(0, n_k, raise_all, jnp.zeros((1, 2 * WIN), F32))
                inverse = jnp.where(valid, 1.0 / total, 0.0)

                def weigh(i, acc):
                    krows, held, bias = k_rows(i)
                    weighted = sc_s[held, :] * inverse
                    one = jnp.sum(weighted[:, :WIN], axis=1, keepdims=True)
                    two = jnp.sum(weighted[:, WIN:], axis=1, keepdims=True)
                    sums = jnp.where(iota((1, 128), 1) < HEAD_DIM, one, two)
                    return acc + jnp.sum(sums * taken(v_ref, krows, LONG, c0).astype(F32), axis=0, keepdims=True)

                ctx_ref[seg, :, c0 : c0 + 128] += lax.fori_loop(0, n_k, weigh, jnp.zeros((1, 128), F32))

    @pl.loop(0, slots + 1)
    def _(seg):
        start = bound_s[seg, 0]
        end = bound_s[seg, 1]
        first = (start // 16) * 16

        @pl.when(end - jnp.minimum(first, length - WIN) > WIN)
        def _():
            @pl.when(end - first <= 256)
            def _():
                long(seg, start, end, 256)

            @pl.when((end - first > 256) & (end - first <= 512))
            def _():
                long(seg, start, end, 512)

            @pl.when(end - first > 512)
            def _():
                longest(seg, start, end)


def exchange_kernel(
    dp, mp, q_ref, k_ref, v_ref, ctx_ref, tok_ref, bound_ref, meta_ref, target_ref, mass_ref, wo_ref, cent_ref,
    docs_ref, out_ref,
    bound_s, ctx_s, part_s, carry_s, got_part, got_carry, tsend, tgot, ss_send, ss_got, csend, cgot, n_send, n_got,
    bound_sem, part_sems, carry_sems, t_sems, ss_sems, c_sems, n_sems,
):
    r = lax.axis_index("dp")
    m = lax.axis_index("mp")
    slots = 32
    cents, width = cent_ref.shape
    to_scalars = pltpu.make_async_copy(bound_ref, bound_s, bound_sem)
    to_scalars.start()

    barrier = pltpu.get_barrier_semaphore()
    nxt = lax.rem(r + 1, dp)
    prv = lax.rem(r + dp - 1, dp)
    for dm in range(1, mp):
        mm = lax.rem(m + dm, mp)
        pl.semaphore_signal(barrier, inc=1, device_id=(r, mm), device_id_type=MESH)
        pl.semaphore_signal(barrier, inc=1, device_id=(nxt, mm), device_id_type=MESH)

    @pl.loop(1, dp)
    def _(d):
        pl.semaphore_signal(barrier, inc=1, device_id=(lax.rem(r + d, dp), m), device_id_type=MESH)

    tsend[...] = target_ref[...].reshape(dp, 1, 128)
    tgot[0] = tsend[0]
    ctx_s[slots + 1 :] = jnp.zeros((SEGS - slots - 1, 1, width), F32)
    to_scalars.wait()
    krow = iota((WIN, 1), 0)
    qlane = iota((1, 2 * WIN), 1) & (WIN - 1)

    def short(seg):
        block = bound_s[seg, 2]
        low = bound_s[seg, 3]
        high = bound_s[seg, 4]
        bias = jnp.where((krow >= low) & (krow < high), 0.0, -1e30)
        valid = (qlane >= low) & (qlane < high)
        q = jnp.concatenate([q_ref[block + i] for i in range(WIN // 16)], axis=0)
        k = jnp.concatenate([k_ref[block + i] for i in range(WIN // 16)], axis=0)
        v = jnp.concatenate([v_ref[block + i] for i in range(WIN // 16)], axis=0)
        for pair in range(width // 128):
            c0 = pair * 128
            q2 = jnp.concatenate([q[:, c0 : c0 + 128], q[:, width + c0 : width + c0 + 128]], axis=0)
            ctx_s[seg, :, c0 : c0 + 128] = ctx_ref[seg, :, c0 : c0 + 128] + block_sums(
                k[:, c0 : c0 + 128], q2, v[:, c0 : c0 + 128], bias, valid
            )

    def to_peer(src, dst, sems, dm):
        mm = lax.rem(m + dm, mp)
        return pltpu.make_async_remote_copy(
            src_ref=src, dst_ref=dst, send_sem=sems.at[0], recv_sem=sems.at[1],
            device_id=(r, mm), device_id_type=MESH,
        )

    def wait_all(buffer, sem):
        pltpu.make_async_copy(buffer, buffer, sem).wait()

    def out_project(rows):
        high, low = halves(rows)
        return jnp.dot(high, wo_ref[...], preferred_element_type=F32) + jnp.dot(
            low, wo_ref[...], preferred_element_type=F32
        )

    groups = (slots + 1) // GROUP

    @pl.loop(0, groups - 1)
    def _(group):
        for j in range(GROUP):
            short(slots - group * GROUP - j)

    carried = out_project(ctx_s[slots:].reshape(SEGS - slots, width))
    row8 = iota((8, width), 0)
    carried_count = meta_ref[8 + slots : 9 + slots, 0:1]
    for mm in range(mp):
        block = carried[:, mm * width : (mm + 1) * width] + jnp.where(m == mm, tok_ref[slots:, :], 0.0)
        carry_s[mm] = jnp.where(row8 == 1, carried_count, block)

    pl.semaphore_wait(barrier, dp - 1 + 2 * (mp - 1))
    for mm in range(mp):
        pltpu.make_async_remote_copy(
            src_ref=carry_s.at[mm], dst_ref=got_carry.at[m], send_sem=carry_sems.at[0],
            recv_sem=carry_sems.at[1], device_id=(prv, mm), device_id_type=MESH,
        ).start()

    @pl.loop(1, dp)
    def _(d):
        pltpu.make_async_remote_copy(
            src_ref=tsend.at[d], dst_ref=tgot.at[dp - d], send_sem=t_sems.at[0], recv_sem=t_sems.at[1],
            device_id=(lax.rem(r + d, dp), m), device_id_type=MESH,
        ).start()

    for j in range(GROUP):
        short(GROUP - 1 - j)

    projected = out_project(ctx_s[:slots].reshape(slots, width))
    for mm in range(mp):
        part_s[mm] = projected[:, mm * width : (mm + 1) * width] + jnp.where(m == mm, tok_ref[:slots, :], 0.0)
    for dm in range(1, mp):
        to_peer(part_s.at[lax.rem(m + dm, mp)], got_part.at[mp - 1 - dm], part_sems, dm).start()

    d_wide = meta_ref[0:1, :]
    rank_wide = meta_ref[1:2, :]
    row = iota((8 * dp, 128), 0)
    col = iota((8 * dp, 128), 1)
    j = row & 7
    pick = (
        ((row >> 3).astype(F32) == d_wide)
        & ((j >> 1).astype(F32) == rank_wide)
        & ((j & 1) == ((col >> 5) & 1))
    )
    pick = jnp.where(pick, 1.0, 0.0).astype(BF16)

    wait_all(got_carry, carry_sems.at[1])
    carry = got_carry[0]
    for i in range(1, mp):
        carry = carry + got_carry[i]
    count_in = got_carry[0][1:2, :]
    counts = meta_ref[8 : 8 + slots, 0:1]
    picks = meta_ref[8 : 8 + slots, 64:65]
    sums = part_s[m] + picks * carry[0:1, :]
    inverse = 1.0 / jnp.maximum(counts + picks * count_in, 1.0)
    wait_all(got_part, part_sems.at[1])
    for i in range(mp - 1):
        sums = sums + got_part[i]
    averages = sums * inverse
    squares = jnp.sum(averages * averages, axis=1, keepdims=True)
    square_row = to_row(squares, slots, 128)
    ss_send[...] = jnp.broadcast_to(square_row, (8, 128))
    for dm in range(1, mp):
        to_peer(ss_send, ss_got.at[mp - 1 - dm], ss_sems, dm).start()
    wait_all(ss_got, ss_sems.at[1])
    for i in range(mp - 1):
        square_row = square_row + ss_got[i][0:1, :]
    eye = iota((slots, 128), 0) == iota((slots, 128), 1)
    squares = jnp.sum(jnp.where(eye, square_row, 0.0), axis=1, keepdims=True)
    vectors = averages * lax.rsqrt(squares * (1.0 / D) + 1e-06)

    high, low = halves(vectors)
    high, low = high.astype(F32), low.astype(F32)
    stacked = jnp.concatenate([high[:, :128], high[:, 128:], low[:, :128], low[:, 128:]], axis=0).astype(BF16)
    outgoing = jnp.dot(pick, stacked, preferred_element_type=F32).reshape(dp, 8, 128)
    csend[...] = outgoing[:, :4, :]
    cgot[0] = csend[0]

    @pl.loop(1, dp)
    def _(d):
        pltpu.make_async_remote_copy(
            src_ref=csend.at[d], dst_ref=cgot.at[dp - d], send_sem=c_sems.at[0], recv_sem=c_sems.at[1],
            device_id=(lax.rem(r + d, dp), m), device_id_type=MESH,
        ).start()

    docs_ref[...] = vectors

    rest = pl.ds(1, dp - 1)
    wait_all(tgot.at[rest], t_sems.at[1])
    tgt_row = jnp.sum(tgot[...], axis=0)
    tgt_col = to_column(tgt_row, 128)
    hits = jnp.where(iota((128, cents), 1).astype(F32) == tgt_col - 1.0, 1.0, 0.0)
    mass = jnp.sum(hits * mass_ref[...], axis=1, keepdims=True)
    hits = hits.astype(BF16)
    cent_high, cent_low = halves(cent_ref[...])
    picked = jnp.dot(hits, cent_high, preferred_element_type=F32) + jnp.dot(
        hits, cent_low, preferred_element_type=F32
    )
    start = mass * picked
    together = jnp.where((tgt_col == tgt_row) & (tgt_row > 0.0), 1.0, 0.0).astype(BF16)
    earlier = iota((128, 128), 0) < iota((128, 128), 1)
    repeats = jnp.sum(jnp.where(earlier & (tgt_col == tgt_row), 1.0, 0.0), axis=0, keepdims=True)
    wanted = jnp.where(repeats == 0.0, tgt_row - 1.0, -1.0)
    writes = jnp.where(iota((cents, 128), 0).astype(F32) == wanted, 1.0, 0.0)
    out_ref[...] = jnp.where(jnp.sum(writes, axis=1, keepdims=True) > 0.0, 0.0, cent_ref[...])
    writes = writes.astype(BF16)

    wait_all(cgot.at[rest], c_sems.at[1])
    arrived = jnp.concatenate(
        [jnp.concatenate([cgot[:, 2 * k, :], cgot[:, 2 * k + 1, :]], axis=1) for k in range(2)], axis=0
    )
    high, low = halves(arrived)
    blended = start + (
        jnp.dot(together, high, preferred_element_type=F32) + jnp.dot(together, low, preferred_element_type=F32)
    )
    norm_row = to_row(jnp.sum(blended * blended, axis=1, keepdims=True), 128, 128)
    n_send[...] = jnp.broadcast_to(norm_row, (8, 128))
    for dm in range(1, mp):
        to_peer(n_send, n_got.at[mp - 1 - dm], n_sems, dm).start()
    wait_all(n_got, n_sems.at[1])
    for i in range(mp - 1):
        norm_row = norm_row + n_got[i][0:1, :]
    norms = to_column(norm_row, 128)
    high, low = halves(blended * lax.rsqrt(norms * (1.0 / D) + 1e-06))
    out_ref[...] += jnp.dot(writes, high, preferred_element_type=F32) + jnp.dot(
        writes, low, preferred_element_type=F32
    )

    wait_all(got_part, part_sems.at[0])
    wait_all(carry_s, carry_sems.at[0])
    wait_all(tsend.at[rest], t_sems.at[0])
    wait_all(ss_got, ss_sems.at[0])
    wait_all(csend.at[rest], c_sems.at[0])
    wait_all(n_got, n_sems.at[0])


def shards(
    tokens, doc_ids, ln_gain, w_query, w_key, w_value, w_out, centroids, cluster_mass, assigned
):
    length = tokens.shape[0]
    width = w_out.shape[0]
    slots = assigned.shape[0]
    cents = centroids.shape[0]
    dp, mp = lax.axis_size("dp"), lax.axis_size("mp")

    def shape(*dims, dtype=F32):
        return jax.ShapeDtypeStruct(dims, dtype)

    vmem = pl.BlockSpec(memory_space=pltpu.VMEM)
    held = pl.pallas_call(
        rows_kernel,
        in_specs=[pl.BlockSpec(memory_space=pltpu.HBM)] * 7,
        out_specs=[vmem] * 8,
        out_shape=[
            shape(length // 16, 16, 2 * width, dtype=BF16),
            shape(length // 16, 16, width, dtype=BF16),
            shape(length // 16, 16, width, dtype=BF16),
            shape(SEGS, 1, width),
            shape(SEGS, width),
            shape(SEGS, 128, dtype=jnp.int32),
            shape(8 + SEGS, 128),
            shape(dp, 128),
        ],
        scratch_shapes=[
            pltpu.VMEM((1, length), jnp.int32),
            pltpu.VMEM((1, slots), jnp.int32),
            pltpu.VMEM((1, D), F32),
            pltpu.VMEM((length, D), BF16),
            pltpu.VMEM((D, 3 * width), BF16),
            pltpu.VMEM((length, D), BF16),
            pltpu.SMEM((SEGS, 128), jnp.int32),
            pltpu.VMEM((length + LONG, 2 * WIN), F32),
            pltpu.SemaphoreType.DMA((6,)),
            pltpu.SemaphoreType.DMA((8,)),
            pltpu.SemaphoreType.DMA,
        ],
        compiler_params=pltpu.CompilerParams(vmem_limit_bytes=40 << 20),
        name="rows",
    )(
        *[pltpu.with_memory_space_constraint(x, pltpu.HBM) for x in (
            doc_ids.reshape(1, length), assigned.reshape(1, slots), ln_gain.reshape(1, D), tokens,
            w_query, w_key, w_value)]
    )

    pair = pltpu.SemaphoreType.DMA((2,))
    return pl.pallas_call(
        functools.partial(exchange_kernel, dp, mp),
        in_specs=[vmem] * 11,
        out_specs=[vmem] * 2,
        out_shape=[shape(slots, width), shape(cents, width)],
        scratch_shapes=[
            pltpu.SMEM((SEGS, 128), jnp.int32),
            pltpu.VMEM((SEGS, 1, width), F32),
            pltpu.VMEM((mp, slots, width), F32),
            pltpu.VMEM((mp, 8, width), F32),
            pltpu.VMEM((mp - 1, slots, width), F32),
            pltpu.VMEM((mp, 8, width), F32),
            pltpu.VMEM((dp, 1, 128), F32),
            pltpu.VMEM((dp, 1, 128), F32),
            pltpu.VMEM((8, 128), F32),
            pltpu.VMEM((mp - 1, 8, 128), F32),
            pltpu.VMEM((dp, 4, 128), F32),
            pltpu.VMEM((dp, 4, 128), F32),
            pltpu.VMEM((8, 128), F32),
            pltpu.VMEM((mp - 1, 8, 128), F32),
            pltpu.SemaphoreType.DMA,
            pair, pair, pair, pair, pair, pair,
        ],
        compiler_params=pltpu.CompilerParams(
            collective_id=0, has_side_effects=True, vmem_limit_bytes=24 << 20
        ),
        name="exchange",
    )(*held, cluster_mass.reshape(1, cents), w_out, centroids)


def solution(mesh):
    placed = (
        P("dp", None),
        P("dp"),
        P(),
        P(None, "mp"),
        P(None, "mp"),
        P(None, "mp"),
        P("mp", None),
        P("dp", "mp"),
        P("dp"),
        P("dp"),
    )
    return jax.shard_map(
        shards,
        mesh=mesh,
        in_specs=placed,
        out_specs=(P("dp", "mp"), P("dp", "mp")),
        check_vma=False,
    )
```

time: 70.3 us -> 47.4 us (0.67)
  Pallas kernels: 61 us -> 45 us
  local copies, waits for them, and re-layouts: 8.12 us -> 1.6 us
    pallas_call x2 -> x1, Pallas kernels: 28.9 us -> 9.36 us  [shards(): pl.pallas_call(rows_kernel, in_specs=[pl.BlockSpec(memory_space=pltpu.HBM...]
    unnamed x24 -> x8, local copies, waits for them, and re-layouts: 8.12 us -> 1.6 us
    pallas_call x1, Pallas kernels: 32.1 us -> 35.7 us  [shards(): pl.pallas_call(functools.partial(exchange_kernel, dp, mp), in_specs=[vmem...]
where the time goes in v2:
time: 47.4 us; the launch traced here: 47.3 us
  Pallas kernels  45 us (95%)
  local copies, waits for them, and re-layouts  1.6 us (3%)
  between operations  0.7 us (1%)
    pallas_call x1, Pallas kernels, shards(): pl.pallas_call(functools.partial(exchange_kernel, dp, mp), in_specs=[vmem...  35.7 us
    pallas_call x1, Pallas kernels, shards(): pl.pallas_call(rows_kernel, in_specs=[pl.BlockSpec(memory_space=pltpu.HBM...  9.36 us
    unnamed x8, local copies, waits for them, and re-layouts  1.6 us

profile of v2, /device:TPU:1, one launch (start us, length us, event | category | flops | bytes accessed | tf_op | source)
XLA Modules:
  0.0 47.3 jit_solution(12503823410681945915)
XLA Ops:
  0.6 0.0 copy-start.2
  0.6 0.0 copy-start
  0.7 0.0 copy-start.1
  0.7 9.4 %rows.1 = (bf16[128,16,512]{2,1,0:T(8,128)(2,1)S(1)}, bf16[128,16,256]{2,1,0:T(8,128)(2,1)S(1)}, bf16[128,16,256]{2,1,0:T(8,128)(2,1)S(1)}, f32[40,1,256]{2,1,0:...) custom-call(s32[1,2048]{1,0:T(1,128)} %bitcast.5, ...), custom_call_target="tpu_custom_call" | custom-call | tf_op jit(solution)/shard_map/rows/pallas_call | solution.py:475
  10.0 0.0 copy-done.2
  10.0 0.0 copy-done
  10.1 0.0 copy-done.1
  10.1 35.7 %exchange.1 = (f32[32,256]{1,0:T(8,128)S(1)}, f32[1024,256]{1,0:T(8,128)S(1)}) custom-call(bf16[128,16,512]{2,1,0:T(8,128)(2,1)S(1)} %get-tuple-element.10.q_ref, bf16[128,16,256]{2,1,0:T(8,128)(2,1)S(1)} %get-tuple-element.11.k_ref, bf16[128,16,256]{2,1,0:T(8,128)(2,1)S(1)} %get-tuple-element.12.v_ref, f32[40,1,256]{2,1,0:T(1,128)S(1)} %get-tuple-element.13.ctx_ref, ...), custom_call_target="tpu_custom_call" | custom-call | tf_op jit(solution)/shard_map/exchange/pallas_call | solution.py:511
  45.8 0.6 %copy.14 = f32[32,256]{1,0:T(8,128)} copy(f32[32,256]{1,0:T(8,128)S(1)} %get-tuple-element.20) | data formatting | bytes 65536
  46.4 1.0 %copy.15 = f32[1024,256]{1,0:T(8,128)} copy(f32[1024,256]{1,0:T(8,128)S(1)} %get-tuple-element.21) | data formatting | bytes 2097152
Async XLA Ops:
  0.6 9.4 %copy-start.2 = (f32[1024]{0:T(1024)S(1)}, f32[1024]{0:T(1024)}, u32[]{:S(2)}) copy-start(f32[1024]{0:T(1024)} %param.18) | copy-start | bytes 12292
  0.6 9.4 %copy-start = (f32[1024,256]{1,0:T(8,128)S(1)}, f32[1024,256]{1,0:T(8,128)}, u32[]{:S(2)}) copy-start(f32[1024,256]{1,0:T(8,128)} %cent_ref.1) | copy-start | bytes 3145732
  0.7 9.4 %copy-start.1 = (bf16[256,1024]{1,0:T(8,128)(2,1)S(1)}, bf16[256,1024]{1,0:T(8,128)(2,1)}, u32[]{:S(2)}) copy-start(bf16[256,1024]{1,0:T(8,128)(2,1)} %wo_ref.1) | copy-start | bytes 1572868

commit v3 on v2

--- a/solution.py
+++ b/solution.py
@@ -13,7 +13,7 @@
 SEGS = 40
 WIN = 128
 LONG = 512
-GROUP = 11
+GROUP = 8
 F32 = jnp.float32
 BF16 = jnp.bfloat16
 MESH = pl.DeviceIdType.MESH
@@ -82,7 +82,37 @@
     ]
     for copy in small + pieces[:2] + weights + pieces[2:]:
         copy.start()
-    for copy in small:
+    small[2].wait()
+
+    gain = gain_v[...]
+    low_half = (iota((1, width), 1) & 127) < HEAD_DIM
+
+    def norm(i):
+        rows = slice(i * piece, (i + 1) * piece)
+        x = tokens_v[rows, :].astype(F32)
+        centered = x - jnp.mean(x, axis=1, keepdims=True)
+        variance = jnp.mean(centered * centered, axis=1, keepdims=True)
+        normed_v[rows, :] = (centered * lax.rsqrt(variance + 1e-05) * gain).astype(BF16)
+
+    def project(at, half):
+        rows = slice(at, at + half)
+        blocks = slice(at // 16, (at + half) // 16)
+        out = jnp.dot(normed_v[rows, :], w_v[...], preferred_element_type=F32)
+        q = out[:, :width]
+        q_ref[blocks, :, 0:width] = jnp.where(low_half, q, 0.0).astype(BF16).reshape(half // 16, 16, width)
+        q_ref[blocks, :, width : 2 * width] = jnp.where(low_half, 0.0, q).astype(BF16).reshape(half // 16, 16, width)
+        k_ref[blocks] = out[:, width : 2 * width].astype(BF16).reshape(half // 16, 16, width)
+        v_ref[blocks] = out[:, 2 * width :].astype(BF16).reshape(half // 16, 16, width)
+
+    qlane = iota((1, 2 * WIN), 1) & (WIN - 1)
+
+    def taken(ref, at, n, c0):
+        return ref[pl.ds(at // 16, n // 16), :, c0 : c0 + 128].reshape(n, 128)
+
+    def queries(at, c0):
+        return jnp.concatenate([taken(q_ref, at, WIN, c0), taken(q_ref, at, WIN, width + c0)], axis=0)
+
+    for copy in small[:2]:
         copy.wait()
 
     local = ids_v[...] - r * slots
@@ -93,14 +123,26 @@
     ends = jnp.sum(jnp.where((own & (local <= seg)) | (carried & (local < 0)), 1.0, 0.0), axis=1, keepdims=True)
     lane = iota((SEGS, 128), 1)
     at_row = jnp.minimum(jnp.floor(starts * (1.0 / 16.0)) * 16.0, float(length - WIN))
-    fits = ends - at_row <= float(WIN)
+    fits = (ends - at_row <= float(WIN)) & (iota((SEGS, 1), 0) < slots)
+    far = jnp.where(fits | ((iota((SEGS, 1), 0) >= slots) & (ends <= float(LONG))), 0.0, 1.0)
+    far = jnp.max(far, axis=0, keepdims=True)
     bound_ref[...] = jnp.where(
         lane == 0,
         starts,
-        jnp.where(lane == 1, ends, jnp.where(lane == 2, at_row * (1.0 / 16.0), jnp.where(lane == 3, starts - at_row, jnp.where(fits, ends, starts) - at_row))),
+        jnp.where(lane == 1, ends, jnp.where(lane == 2, at_row * (1.0 / 16.0), jnp.where(lane == 3, starts - at_row, jnp.where(lane == 4, jnp.where(fits, ends, starts) - at_row, far)))),
     ).astype(jnp.int32)
     to_scalars = pltpu.make_async_copy(bound_ref, bound_s, bound_sem)
     to_scalars.start()
+    ctx_ref[...] = jnp.zeros_like(ctx_ref)
+
+    for i in range(parts // 2):
+        pieces[i].wait()
+        norm(i)
+    for copy in weights + pieces[parts // 2 :]:
+        copy.wait()
+    project(0, length // 2)
+    for i in range(parts // 2, parts):
+        norm(i)
     counts = ends - starts
     picks = jnp.where((ends == float(length)) & (starts < float(length)), 1.0, 0.0)
     meta_ref[8:, :] = jnp.where(lane < 64, counts, picks)
@@ -124,38 +166,19 @@
     d_wide = jnp.sum(jnp.where(pick, d_col, 0.0), axis=0, keepdims=True)
     rank_wide = jnp.sum(jnp.where(pick, rank_col, 0.0), axis=0, keepdims=True)
     meta_ref[:8, :] = jnp.where(iota((8, 128), 0) == 0, d_wide, rank_wide)
-    ctx_ref[...] = jnp.zeros_like(ctx_ref)
-
-    half = length // 2
-    gain = gain_v[...]
-    low_half = (iota((half, width), 1) & 127) < HEAD_DIM
-
-    def norm(i):
-        rows = slice(i * piece, (i + 1) * piece)
-        x = tokens_v[rows, :].astype(F32)
-        centered = x - jnp.mean(x, axis=1, keepdims=True)
-        variance = jnp.mean(centered * centered, axis=1, keepdims=True)
-        normed_v[rows, :] = (centered * lax.rsqrt(variance + 1e-05) * gain).astype(BF16)
-
-    def project(i):
-        rows = slice(i * half, (i + 1) * half)
-        blocks = slice(i * half // 16, (i + 1) * half // 16)
-        out = jnp.dot(normed_v[rows, :], w_v[...], preferred_element_type=F32)
-        q = out[:, :width]
-        q_ref[blocks, :, 0:width] = jnp.where(low_half, q, 0.0).astype(BF16).reshape(half // 16, 16, width)
-        q_ref[blocks, :, width : 2 * width] = jnp.where(low_half, 0.0, q).astype(BF16).reshape(half // 16, 16, width)
-        k_ref[blocks] = out[:, width : 2 * width].astype(BF16).reshape(half // 16, 16, width)
-        v_ref[blocks] = out[:, 2 * width :].astype(BF16).reshape(half // 16, 16, width)
-
-    for i in range(parts // 2):
-        pieces[i].wait()
-        norm(i)
-    for copy in weights + pieces[parts // 2 :]:
-        copy.wait()
-    project(0)
-    for i in range(parts // 2, parts):
-        norm(i)
-    project(1)
+    carried_end = jnp.where(ends[slots:slots + 1] <= float(LONG), ends[slots:slots + 1], 0.0).astype(jnp.int32)
+    carried_bias = jnp.where(iota((LONG, 1), 0) < carried_end, 0.0, -1e30)
+    for pair in range(width // 128):
+        c0 = pair * 128
+        total = jnp.zeros((1, 128), F32)
+        for i in range(LONG // WIN):
+            total = total + block_sums(
+                taken(k_ref, 0, LONG, c0), queries(i * WIN, c0), taken(v_ref, 0, LONG, c0),
+                carried_bias, qlane < carried_end - i * WIN,
+            )
+        ctx_ref[slots, :, c0 : c0 + 128] = total
+
+    project(length // 2, length // 2)
 
     seg_of = jnp.where(local < 0, slots, local)
     member = jnp.where(seg == seg_of, 1.0, 0.0).astype(BF16)
@@ -163,14 +186,6 @@
     tok_ref[...] = jnp.dot(member, tokens_v[:, columns], preferred_element_type=F32)
 
     to_scalars.wait()
-    qlane = iota((1, 2 * WIN), 1) & (WIN - 1)
-
-    def taken(ref, at, n, c0):
-        return ref[pl.ds(at // 16, n // 16), :, c0 : c0 + 128].reshape(n, 128)
-
-    def queries(at, c0):
-        return jnp.concatenate([taken(q_ref, at, WIN, c0), taken(q_ref, at, WIN, width + c0)], axis=0)
-
     def long(seg, start, end, reach):
         first = (start // 16) * 16
         base = pl.multiple_of(jnp.minimum(first, length - reach), 16)
@@ -235,25 +250,27 @@
 
                 ctx_ref[seg, :, c0 : c0 + 128] += lax.fori_loop(0, n_k, weigh, jnp.zeros((1, 128), F32))
 
-    @pl.loop(0, slots + 1)
-    def _(seg):
-        start = bound_s[seg, 0]
-        end = bound_s[seg, 1]
-        first = (start // 16) * 16
-
-        @pl.when(end - jnp.minimum(first, length - WIN) > WIN)
-        def _():
-            @pl.when(end - first <= 256)
+    @pl.when(bound_s[0, 5] > 0)
+    def _():
+        @pl.loop(0, slots + 1)
+        def _(seg):
+            start = bound_s[seg, 0]
+            end = bound_s[seg, 1]
+            first = (start // 16) * 16
+
+            @pl.when((end - jnp.minimum(first, length - WIN) > WIN) & ((seg < slots) | (end > LONG)))
             def _():
-                long(seg, start, end, 256)
-
-            @pl.when((end - first > 256) & (end - first <= 512))
-            def _():
-                long(seg, start, end, 512)
-
-            @pl.when(end - first > 512)
-            def _():
-                longest(seg, start, end)
+                @pl.when(end - first <= 256)
+                def _():
+                    long(seg, start, end, 256)
+
+                @pl.when((end - first > 256) & (end - first <= 512))
+                def _():
+                    long(seg, start, end, 512)
+
+                @pl.when(end - first > 512)
+                def _():
+                    longest(seg, start, end)
 
 
 def exchange_kernel(
@@ -320,19 +337,19 @@
             low, wo_ref[...], preferred_element_type=F32
         )
 
-    groups = (slots + 1) // GROUP
-
-    @pl.loop(0, groups - 1)
+    @pl.loop(0, slots // GROUP)
     def _(group):
         for j in range(GROUP):
-            short(slots - group * GROUP - j)
-
-    carried = out_project(ctx_s[slots:].reshape(SEGS - slots, width))
+            short(group * GROUP + j)
+
+    ctx_s[slots] = ctx_ref[slots]
+    projected = out_project(ctx_s[...].reshape(SEGS, width))
     row8 = iota((8, width), 0)
     carried_count = meta_ref[8 + slots : 9 + slots, 0:1]
     for mm in range(mp):
-        block = carried[:, mm * width : (mm + 1) * width] + jnp.where(m == mm, tok_ref[slots:, :], 0.0)
-        carry_s[mm] = jnp.where(row8 == 1, carried_count, block)
+        block = projected[:, mm * width : (mm + 1) * width] + jnp.where(m == mm, tok_ref[...], 0.0)
+        part_s[mm] = block[:slots]
+        carry_s[mm] = jnp.where(row8 == 1, carried_count, block[slots:])
 
     pl.semaphore_wait(barrier, dp - 1 + 2 * (mp - 1))
     for mm in range(mp):
@@ -340,6 +357,8 @@
             src_ref=carry_s.at[mm], dst_ref=got_carry.at[m], send_sem=carry_sems.at[0],
             recv_sem=carry_sems.at[1], device_id=(prv, mm), device_id_type=MESH,
         ).start()
+    for dm in range(1, mp):
+        to_peer(part_s.at[lax.rem(m + dm, mp)], got_part.at[mp - 1 - dm], part_sems, dm).start()
 
     @pl.loop(1, dp)
     def _(d):
@@ -347,15 +366,6 @@
             src_ref=tsend.at[d], dst_ref=tgot.at[dp - d], send_sem=t_sems.at[0], recv_sem=t_sems.at[1],
             device_id=(lax.rem(r + d, dp), m), device_id_type=MESH,
         ).start()
-
-    for j in range(GROUP):
-        short(GROUP - 1 - j)
-
-    projected = out_project(ctx_s[:slots].reshape(slots, width))
-    for mm in range(mp):
-        part_s[mm] = projected[:, mm * width : (mm + 1) * width] + jnp.where(m == mm, tok_ref[:slots, :], 0.0)
-    for dm in range(1, mp):
-        to_peer(part_s.at[lax.rem(m + dm, mp)], got_part.at[mp - 1 - dm], part_sems, dm).start()
 
     d_wide = meta_ref[0:1, :]
     rank_wide = meta_ref[1:2, :]

time: 47.4 us -> 43.8 us (0.924)
  Pallas kernels: 45 us -> 41.5 us
    pallas_call x1, Pallas kernels: 35.7 us -> 33 us  [shards(): pl.pallas_call(functools.partial(exchange_kernel, dp, mp), in_specs=[vmem...]
    pallas_call x1, Pallas kernels: 9.36 us -> 8.4 us  [shards(): pl.pallas_call(rows_kernel, in_specs=[pl.BlockSpec(memory_space=pltpu.HBM...]
where the time goes in v3:
time: 43.8 us; the launch traced here: 43.7 us
  Pallas kernels  41.5 us (95%)
  local copies, waits for them, and re-layouts  1.6 us (4%)
  between operations  0.7 us (2%)
    pallas_call x1, Pallas kernels, shards(): pl.pallas_call(functools.partial(exchange_kernel, dp, mp), in_specs=[vmem...  33 us
    pallas_call x1, Pallas kernels, shards(): pl.pallas_call(rows_kernel, in_specs=[pl.BlockSpec(memory_space=pltpu.HBM...  8.4 us
    unnamed x8, local copies, waits for them, and re-layouts  1.6 us

profile of v3, /device:TPU:1, one launch (start us, length us, event | category | flops | bytes accessed | tf_op | source)
XLA Modules:
  0.0 43.7 jit_solution(2868464397310923338)
XLA Ops:
  0.6 0.0 copy-start.2
  0.6 0.0 copy-start
  0.7 0.0 copy-start.1
  0.7 8.4 %rows.1 = (bf16[128,16,512]{2,1,0:T(8,128)(2,1)S(1)}, bf16[128,16,256]{2,1,0:T(8,128)(2,1)S(1)}, bf16[128,16,256]{2,1,0:T(8,128)(2,1)S(1)}, f32[40,1,256]{2,1,0:...) custom-call(s32[1,2048]{1,0:T(1,128)} %bitcast.5, ...), custom_call_target="tpu_custom_call" | custom-call | tf_op jit(solution)/shard_map/rows/pallas_call | solution.py:485
  9.1 0.0 copy-done.2
  9.1 0.0 copy-done
  9.1 0.0 copy-done.1
  9.1 33.0 %exchange.1 = (f32[32,256]{1,0:T(8,128)S(1)}, f32[1024,256]{1,0:T(8,128)S(1)}) custom-call(bf16[128,16,512]{2,1,0:T(8,128)(2,1)S(1)} %get-tuple-element.10.q_ref, bf16[128,16,256]{2,1,0:T(8,128)(2,1)S(1)} %get-tuple-element.11.k_ref, bf16[128,16,256]{2,1,0:T(8,128)(2,1)S(1)} %get-tuple-element.12.v_ref, f32[40,1,256]{2,1,0:T(1,128)S(1)} %get-tuple-element.13.ctx_ref, ...), custom_call_target="tpu_custom_call" | custom-call | tf_op jit(solution)/shard_map/exchange/pallas_call | solution.py:521
  42.2 0.6 %copy.14 = f32[32,256]{1,0:T(8,128)} copy(f32[32,256]{1,0:T(8,128)S(1)} %get-tuple-element.20) | data formatting | bytes 65536
  42.8 1.0 %copy.15 = f32[1024,256]{1,0:T(8,128)} copy(f32[1024,256]{1,0:T(8,128)S(1)} %get-tuple-element.21) | data formatting | bytes 2097152
Async XLA Ops:
  0.6 8.4 %copy-start.2 = (f32[1024]{0:T(1024)S(1)}, f32[1024]{0:T(1024)}, u32[]{:S(2)}) copy-start(f32[1024]{0:T(1024)} %param.18) | copy-start | bytes 12292
  0.6 8.4 %copy-start = (f32[1024,256]{1,0:T(8,128)S(1)}, f32[1024,256]{1,0:T(8,128)}, u32[]{:S(2)}) copy-start(f32[1024,256]{1,0:T(8,128)} %cent_ref.1) | copy-start | bytes 3145732
  0.7 8.4 %copy-start.1 = (bf16[256,1024]{1,0:T(8,128)(2,1)S(1)}, bf16[256,1024]{1,0:T(8,128)(2,1)}, u32[]{:S(2)}) copy-start(bf16[256,1024]{1,0:T(8,128)(2,1)} %wo_ref.1) | copy-start | bytes 1572868

commit v4 on v3

--- a/solution.py
+++ b/solution.py
@@ -275,9 +275,9 @@
 
 def exchange_kernel(
     dp, mp, q_ref, k_ref, v_ref, ctx_ref, tok_ref, bound_ref, meta_ref, target_ref, mass_ref, wo_ref, cent_ref,
-    docs_ref, out_ref,
+    docs_ref, rows_ref, writes_ref, keep_ref,
     bound_s, ctx_s, part_s, carry_s, got_part, got_carry, tsend, tgot, ss_send, ss_got, csend, cgot, n_send, n_got,
-    bound_sem, part_sems, carry_sems, t_sems, ss_sems, c_sems, n_sems,
+    ready, bound_sem, part_sems, carry_sems, t_sems, ss_sems, c_sems, n_sems,
 ):
     r = lax.axis_index("dp")
     m = lax.axis_index("mp")
@@ -289,14 +289,22 @@
     barrier = pltpu.get_barrier_semaphore()
     nxt = lax.rem(r + 1, dp)
     prv = lax.rem(r + dp - 1, dp)
+    plane = 8
+    layers = dp // plane
+    mine = lax.rem(r, plane)
+
+    def along_z(i):
+        return lax.rem(r + i * plane, dp)
+
     for dm in range(1, mp):
-        mm = lax.rem(m + dm, mp)
-        pl.semaphore_signal(barrier, inc=1, device_id=(r, mm), device_id_type=MESH)
+        pl.semaphore_signal(barrier, inc=1, device_id=(r, lax.rem(m + dm, mp)), device_id_type=MESH)
+    for mm in range(mp):
         pl.semaphore_signal(barrier, inc=1, device_id=(nxt, mm), device_id_type=MESH)
-
-    @pl.loop(1, dp)
-    def _(d):
-        pl.semaphore_signal(barrier, inc=1, device_id=(lax.rem(r + d, dp), m), device_id_type=MESH)
+    for i in range(1, layers):
+        pl.semaphore_signal(barrier, inc=1, device_id=(along_z(i), m), device_id_type=MESH)
+    for i in range(1, plane):
+        peer = r - mine + lax.rem(mine + i, plane)
+        pl.semaphore_signal(barrier, inc=1, device_id=(peer, m), device_id_type=MESH)
 
     tsend[...] = target_ref[...].reshape(dp, 1, 128)
     tgot[0] = tsend[0]
@@ -351,7 +359,7 @@
         part_s[mm] = block[:slots]
         carry_s[mm] = jnp.where(row8 == 1, carried_count, block[slots:])
 
-    pl.semaphore_wait(barrier, dp - 1 + 2 * (mp - 1))
+    pl.semaphore_wait(barrier, mp - 1 + mp + layers - 1 + plane - 1)
     for mm in range(mp):
         pltpu.make_async_remote_copy(
             src_ref=carry_s.at[mm], dst_ref=got_carry.at[m], send_sem=carry_sems.at[0],
@@ -360,12 +368,8 @@
     for dm in range(1, mp):
         to_peer(part_s.at[lax.rem(m + dm, mp)], got_part.at[mp - 1 - dm], part_sems, dm).start()
 
-    @pl.loop(1, dp)
-    def _(d):
-        pltpu.make_async_remote_copy(
-            src_ref=tsend.at[d], dst_ref=tgot.at[dp - d], send_sem=t_sems.at[0], recv_sem=t_sems.at[1],
-            device_id=(lax.rem(r + d, dp), m), device_id_type=MESH,
-        ).start()
+    for i in range(1, layers):
+        pl.semaphore_signal(ready, inc=1, device_id=(along_z(i), m), device_id_type=MESH)
 
     d_wide = meta_ref[0:1, :]
     rank_wide = meta_ref[1:2, :]
@@ -397,6 +401,15 @@
     ss_send[...] = jnp.broadcast_to(square_row, (8, 128))
     for dm in range(1, mp):
         to_peer(ss_send, ss_got.at[mp - 1 - dm], ss_sems, dm).start()
+    pl.semaphore_wait(ready, layers - 1)
+
+    @pl.loop(1, dp)
+    def _(d):
+        pltpu.make_async_remote_copy(
+            src_ref=tsend.at[d], dst_ref=tgot.at[dp - d], send_sem=t_sems.at[0], recv_sem=t_sems.at[1],
+            device_id=(lax.rem(r + d, dp), m), device_id_type=MESH,
+        ).start()
+
     wait_all(ss_got, ss_sems.at[1])
     for i in range(mp - 1):
         square_row = square_row + ss_got[i][0:1, :]
@@ -437,8 +450,8 @@
     repeats = jnp.sum(jnp.where(earlier & (tgt_col == tgt_row), 1.0, 0.0), axis=0, keepdims=True)
     wanted = jnp.where(repeats == 0.0, tgt_row - 1.0, -1.0)
     writes = jnp.where(iota((cents, 128), 0).astype(F32) == wanted, 1.0, 0.0)
-    out_ref[...] = jnp.where(jnp.sum(writes, axis=1, keepdims=True) > 0.0, 0.0, cent_ref[...])
-    writes = writes.astype(BF16)
+    keep_ref[...] = jnp.where(jnp.sum(writes, axis=1, keepdims=True) > 0.0, 0.0, cent_ref[...])
+    writes_ref[...] = writes.astype(BF16)
 
     wait_all(cgot.at[rest], c_sems.at[1])
     arrived = jnp.concatenate(
@@ -456,10 +469,7 @@
     for i in range(mp - 1):
         norm_row = norm_row + n_got[i][0:1, :]
     norms = to_column(norm_row, 128)
-    high, low = halves(blended * lax.rsqrt(norms * (1.0 / D) + 1e-06))
-    out_ref[...] += jnp.dot(writes, high, preferred_element_type=F32) + jnp.dot(
-        writes, low, preferred_element_type=F32
-    )
+    rows_ref[...] = blended * lax.rsqrt(norms * (1.0 / D) + 1e-06)
 
     wait_all(got_part, part_sems.at[0])
     wait_all(carry_s, carry_sems.at[0])
@@ -467,6 +477,28 @@
     wait_all(ss_got, ss_sems.at[0])
     wait_all(csend.at[rest], c_sems.at[0])
     wait_all(n_got, n_sems.at[0])
+
+
+def write_kernel(docs_ref, rows_ref, writes_ref, keep_ref, docs_hbm, out_hbm, out_v, sems):
+    parts = 4
+    block = keep_ref.shape[0] // parts
+    docs_copy = pltpu.make_async_copy(docs_ref, docs_hbm, sems.at[parts])
+    docs_copy.start()
+    high, low = halves(rows_ref[...])
+    copies = []
+    for i in range(parts):
+        rows = pl.ds(i * block, block)
+        writes = writes_ref[rows, :]
+        out_v[rows, :] = (
+            keep_ref[rows, :]
+            + jnp.dot(writes, high, preferred_element_type=F32)
+            + jnp.dot(writes, low, preferred_element_type=F32)
+        )
+        copies.append(pltpu.make_async_copy(out_v.at[rows], out_hbm.at[rows], sems.at[i]))
+        copies[-1].start()
+    docs_copy.wait()
+    for copy in copies:
+        copy.wait()
 
 
 def shards(
@@ -518,11 +550,16 @@
     )
 
     pair = pltpu.SemaphoreType.DMA((2,))
-    return pl.pallas_call(
+    new = pl.pallas_call(
         functools.partial(exchange_kernel, dp, mp),
         in_specs=[vmem] * 11,
-        out_specs=[vmem] * 2,
-        out_shape=[shape(slots, width), shape(cents, width)],
+        out_specs=[vmem] * 4,
+        out_shape=[
+            shape(slots, width),
+            shape(128, width),
+            shape(cents, 128, dtype=BF16),
+            shape(cents, width),
+        ],
         scratch_shapes=[
             pltpu.SMEM((SEGS, 128), jnp.int32),
             pltpu.VMEM((SEGS, 1, width), F32),
@@ -538,6 +575,7 @@
             pltpu.VMEM((dp, 4, 128), F32),
             pltpu.VMEM((8, 128), F32),
             pltpu.VMEM((mp - 1, 8, 128), F32),
+            pltpu.SemaphoreType.REGULAR,
             pltpu.SemaphoreType.DMA,
             pair, pair, pair, pair, pair, pair,
         ],
@@ -546,6 +584,17 @@
         ),
         name="exchange",
     )(*held, cluster_mass.reshape(1, cents), w_out, centroids)
+
+    anywhere = pl.BlockSpec(memory_space=pl.ANY)
+    return pl.pallas_call(
+        write_kernel,
+        in_specs=[vmem] * 4,
+        out_specs=[anywhere] * 2,
+        out_shape=[shape(slots, width), shape(cents, width)],
+        scratch_shapes=[pltpu.VMEM((cents, width), F32), pltpu.SemaphoreType.DMA((5,))],
+        compiler_params=pltpu.CompilerParams(vmem_limit_bytes=16 << 20),
+        name="write",
+    )(*new)
 
 
 def solution(mesh):

time: 43.8 us -> 43.2 us (0.986)
  local copies, waits for them, and re-layouts: 1.6 us -> 0.01 us
  Pallas kernels: 41.5 us -> 42.4 us
    unnamed x8 -> x6, local copies, waits for them, and re-layouts: 1.6 us -> 0.01 us
    pallas_call x0 -> x1, Pallas kernels: none -> 1.29 us  [shards(): pl.pallas_call(write_kernel, in_specs=[vmem] * 4, out_specs=[anywhere] *...]
where the time goes in v4:
time: 43.2 us; the launch traced here: 43.1 us
  Pallas kernels  42.4 us (98%)
  between operations  0.7 us (2%)
    pallas_call x1, Pallas kernels, shards(): pl.pallas_call(functools.partial(exchange_kernel, dp, mp), in_specs=[vmem...  32.7 us
    pallas_call x1, Pallas kernels, shards(): pl.pallas_call(rows_kernel, in_specs=[pl.BlockSpec(memory_space=pltpu.HBM...  8.4 us
    pallas_call x1, Pallas kernels, shards(): pl.pallas_call(write_kernel, in_specs=[vmem] * 4, out_specs=[anywhere] *...  1.29 us

profile of v4, /device:TPU:1, one launch (start us, length us, event | category | flops | bytes accessed | tf_op | source)
XLA Modules:
  0.0 43.1 jit_solution(17872567720637295455)
XLA Ops:
  0.6 0.0 copy-start.2
  0.6 0.0 copy-start
  0.7 0.0 copy-start.1
  0.7 8.4 %rows.1 = (bf16[128,16,512]{2,1,0:T(8,128)(2,1)S(1)}, bf16[128,16,256]{2,1,0:T(8,128)(2,1)S(1)}, bf16[128,16,256]{2,1,0:T(8,128)(2,1)S(1)}, f32[40,1,256]{2,1,0:...) custom-call(s32[1,2048]{1,0:T(1,128)} %bitcast.5, ...), custom_call_target="tpu_custom_call" | custom-call | tf_op jit(solution)/shard_map/rows/pallas_call | solution.py:517
  9.1 0.0 copy-done.2
  9.1 0.0 copy-done
  9.1 0.0 copy-done.1
  9.1 32.7 %exchange.1 = (f32[32,256]{1,0:T(8,128)S(1)}, f32[128,256]{1,0:T(8,128)S(1)}, bf16[1024,128]{1,0:T(8,128)(2,1)S(1)}, f32[1024,256]{1,0:T(8,128)S(1)}) custom-call(bf16[128,16,512]{2,1,0:T(8,128)(2,1)S(1)} %get-tuple-element.14.q_ref, bf16[128,16,256]{2,1,0:T(8,128)(2,1)S(1)} %get-tuple-element.15.k_ref, bf16[128,16,256]{2,1,0:T(8,128)(2,1)S(1)} %get-tuple-element.16.v_ref, ...), custom_call_target="tpu_custom_call" | custom-call | tf_op jit(solution)/shard_map/exchange/pallas_call | solution.py:553
  41.8 1.3 %write.1 = (f32[32,256]{1,0:T(8,128)}, f32[1024,256]{1,0:T(8,128)}) custom-call(f32[32,256]{1,0:T(8,128)S(1)} %get-tuple-element.22.docs_ref, f32[128,256]{1,0:T(8,128)S(1)} %get-tuple-element.23.rows_ref, bf16[1024,128]{1,0:T(8,128)(2,1)S(1)} %get-tuple-element.24.writes_ref, f32[1024,256]{1,0:T(8,128)S(1)} %get-tuple-element.25.keep_ref), custom_call_target="tpu_custom_call" | custom-call | tf_op jit(solution)/shard_map/write/pallas_call | solution.py:589
Async XLA Ops:
  0.6 8.4 %copy-start.2 = (f32[1024]{0:T(1024)S(1)}, f32[1024]{0:T(1024)}, u32[]{:S(2)}) copy-start(f32[1024]{0:T(1024)} %param.18) | copy-start | bytes 12292
  0.6 8.4 %copy-start = (f32[1024,256]{1,0:T(8,128)S(1)}, f32[1024,256]{1,0:T(8,128)}, u32[]{:S(2)}) copy-start(f32[1024,256]{1,0:T(8,128)} %cent_ref.1) | copy-start | bytes 3145732
  0.7 8.4 %copy-start.1 = (bf16[256,1024]{1,0:T(8,128)(2,1)S(1)}, bf16[256,1024]{1,0:T(8,128)(2,1)}, u32[]{:S(2)}) copy-start(bf16[256,1024]{1,0:T(8,128)(2,1)} %wo_ref.1) | copy-start | bytes 1572868

commit v5 on v4

--- a/solution.py
+++ b/solution.py
@@ -13,7 +13,7 @@
 SEGS = 40
 WIN = 128
 LONG = 512
-GROUP = 8
+GROUP = 16
 F32 = jnp.float32
 BF16 = jnp.bfloat16
 MESH = pl.DeviceIdType.MESH
@@ -274,15 +274,19 @@
 
 
 def exchange_kernel(
-    dp, mp, q_ref, k_ref, v_ref, ctx_ref, tok_ref, bound_ref, meta_ref, target_ref, mass_ref, wo_ref, cent_ref,
+    dp, mp, q_ref, k_ref, v_ref, ctx_ref, tok_ref, bound_ref, meta_ref, target_ref, mass_ref, wo_hbm, cent_hbm,
     docs_ref, rows_ref, writes_ref, keep_ref,
     bound_s, ctx_s, part_s, carry_s, got_part, got_carry, tsend, tgot, ss_send, ss_got, csend, cgot, n_send, n_got,
-    ready, bound_sem, part_sems, carry_sems, t_sems, ss_sems, c_sems, n_sems,
+    wo_ref, cent_ref, ready, late_sems, bound_sem, part_sems, carry_sems, t_sems, ss_sems, c_sems, n_sems,
 ):
     r = lax.axis_index("dp")
     m = lax.axis_index("mp")
     slots = 32
     cents, width = cent_ref.shape
+    load_wo = pltpu.make_async_copy(wo_hbm, wo_ref, late_sems.at[0])
+    load_cent = pltpu.make_async_copy(cent_hbm, cent_ref, late_sems.at[1])
+    load_wo.start()
+    load_cent.start()
     to_scalars = pltpu.make_async_copy(bound_ref, bound_s, bound_sem)
     to_scalars.start()
 
@@ -336,6 +340,13 @@
             device_id=(r, mm), device_id_type=MESH,
         )
 
+    def far_first(i):
+        def order(k):
+            odd = k % 2
+            return 4 - odd * ((k + 1) // 2) + (1 - odd) * (k // 2)
+
+        return order(i // 8) * 8 + order(i % 8)
+
     def wait_all(buffer, sem):
         pltpu.make_async_copy(buffer, buffer, sem).wait()
 
@@ -351,6 +362,7 @@
             short(group * GROUP + j)
 
     ctx_s[slots] = ctx_ref[slots]
+    load_wo.wait()
     projected = out_project(ctx_s[...].reshape(SEGS, width))
     row8 = iota((8, width), 0)
     carried_count = meta_ref[8 + slots : 9 + slots, 0:1]
@@ -424,8 +436,9 @@
     csend[...] = outgoing[:, :4, :]
     cgot[0] = csend[0]
 
-    @pl.loop(1, dp)
-    def _(d):
+    @pl.loop(0, dp - 1)
+    def _(i):
+        d = far_first(i)
         pltpu.make_async_remote_copy(
             src_ref=csend.at[d], dst_ref=cgot.at[dp - d], send_sem=c_sems.at[0], recv_sem=c_sems.at[1],
             device_id=(lax.rem(r + d, dp), m), device_id_type=MESH,
@@ -440,6 +453,7 @@
     hits = jnp.where(iota((128, cents), 1).astype(F32) == tgt_col - 1.0, 1.0, 0.0)
     mass = jnp.sum(hits * mass_ref[...], axis=1, keepdims=True)
     hits = hits.astype(BF16)
+    load_cent.wait()
     cent_high, cent_low = halves(cent_ref[...])
     picked = jnp.dot(hits, cent_high, preferred_element_type=F32) + jnp.dot(
         hits, cent_low, preferred_element_type=F32
@@ -552,7 +566,7 @@
     pair = pltpu.SemaphoreType.DMA((2,))
     new = pl.pallas_call(
         functools.partial(exchange_kernel, dp, mp),
-        in_specs=[vmem] * 11,
+        in_specs=[vmem] * 9 + [pl.BlockSpec(memory_space=pl.ANY)] * 2,
         out_specs=[vmem] * 4,
         out_shape=[
             shape(slots, width),
@@ -575,7 +589,10 @@
             pltpu.VMEM((dp, 4, 128), F32),
             pltpu.VMEM((8, 128), F32),
             pltpu.VMEM((mp - 1, 8, 128), F32),
+            pltpu.VMEM((width, D), BF16),
+            pltpu.VMEM((cents, width), F32),
             pltpu.SemaphoreType.REGULAR,
+            pltpu.SemaphoreType.DMA((2,)),
             pltpu.SemaphoreType.DMA,
             pair, pair, pair, pair, pair, pair,
         ],
@@ -583,7 +600,8 @@
             collective_id=0, has_side_effects=True, vmem_limit_bytes=24 << 20
         ),
         name="exchange",
-    )(*held, cluster_mass.reshape(1, cents), w_out, centroids)
+    )(*held, cluster_mass.reshape(1, cents),
+        *[pltpu.with_memory_space_constraint(x, pltpu.HBM) for x in (w_out, centroids)])
 
     anywhere = pl.BlockSpec(memory_space=pl.ANY)
     return pl.pallas_call(

time: 43.2 us -> 42.4 us (0.981)
  Pallas kernels: 42.4 us -> 41.5 us
    pallas_call x1, Pallas kernels: 32.7 us -> 31.7 us  [shards(): pl.pallas_call(functools.partial(exchange_kernel, dp, mp), in_specs=[vmem...]
where the time goes in v5:
time: 42.4 us; the launch traced here: 42.3 us
  Pallas kernels  41.5 us (98%)
  between operations  0.82 us (2%)
    pallas_call x1, Pallas kernels, shards(): pl.pallas_call(functools.partial(exchange_kernel, dp, mp), in_specs=[vmem...  31.7 us
    pallas_call x1, Pallas kernels, shards(): pl.pallas_call(rows_kernel, in_specs=[pl.BlockSpec(memory_space=pltpu.HBM...  8.46 us
    pallas_call x1, Pallas kernels, shards(): pl.pallas_call(write_kernel, in_specs=[vmem] * 4, out_specs=[anywhere] *...  1.29 us

profile of v5, /device:TPU:1, one launch (start us, length us, event | category | flops | bytes accessed | tf_op | source)
XLA Modules:
  0.0 42.3 jit_solution(1636251418113863483)
XLA Ops:
  0.6 0.0 copy-start
  0.6 8.5 %rows.1 = (bf16[128,16,512]{2,1,0:T(8,128)(2,1)S(1)}, bf16[128,16,256]{2,1,0:T(8,128)(2,1)S(1)}, bf16[128,16,256]{2,1,0:T(8,128)(2,1)S(1)}, f32[40,1,256]{2,1,0:...) custom-call(s32[1,2048]{1,0:T(1,128)} %bitcast.5, ...), custom_call_target="tpu_custom_call" | custom-call | tf_op jit(solution)/shard_map/rows/pallas_call | solution.py:531
  9.1 0.0 copy-done
  9.1 31.7 %exchange.1 = (f32[32,256]{1,0:T(8,128)S(1)}, f32[128,256]{1,0:T(8,128)S(1)}, bf16[1024,128]{1,0:T(8,128)(2,1)S(1)}, f32[1024,256]{1,0:T(8,128)S(1)}) custom-call(bf16[128,16,512]{2,1,0:T(8,128)(2,1)S(1)} %get-tuple-element.14.q_ref, bf16[128,16,256]{2,1,0:T(8,128)(2,1)S(1)} %get-tuple-element.15.k_ref, bf16[128,16,256]{2,1,0:T(8,128)(2,1)S(1)} %get-tuple-element.16.v_ref, ...), custom_call_target="tpu_custom_call" | custom-call | tf_op jit(solution)/shard_map/exchange/pallas_call | solution.py:567
  40.9 1.3 %write.1 = (f32[32,256]{1,0:T(8,128)}, f32[1024,256]{1,0:T(8,128)}) custom-call(f32[32,256]{1,0:T(8,128)S(1)} %get-tuple-element.22.docs_ref, f32[128,256]{1,0:T(8,128)S(1)} %get-tuple-element.23.rows_ref, bf16[1024,128]{1,0:T(8,128)(2,1)S(1)} %get-tuple-element.24.writes_ref, f32[1024,256]{1,0:T(8,128)S(1)} %get-tuple-element.25.keep_ref), custom_call_target="tpu_custom_call" | custom-call | tf_op jit(solution)/shard_map/write/pallas_call | solution.py:607
Async XLA Ops:
  0.6 8.5 %copy-start = (f32[1024]{0:T(1024)S(1)}, f32[1024]{0:T(1024)}, u32[]{:S(2)}) copy-start(f32[1024]{0:T(1024)} %param.18) | copy-start | bytes 12292

commit v6 on v5

--- a/solution.py
+++ b/solution.py
@@ -13,7 +13,7 @@
 SEGS = 40
 WIN = 128
 LONG = 512
-GROUP = 16
+GROUP = 8
 F32 = jnp.float32
 BF16 = jnp.bfloat16
 MESH = pl.DeviceIdType.MESH
@@ -55,7 +55,7 @@
 
 def rows_kernel(
     ids_hbm, assigned_hbm, gain_hbm, tokens_hbm, wq_hbm, wk_hbm, wv_hbm,
-    q_ref, k_ref, v_ref, ctx_ref, tok_ref, bound_ref, meta_ref, target_ref,
+    q_ref, k_ref, v_ref, ctx_ref, bound_ref, meta_ref, target_ref,
     ids_v, assigned_v, gain_v, tokens_v, w_v, normed_v, bound_s, sc_s, sems, token_sems, bound_sem,
 ):
     length = q_ref.shape[0] * 16
@@ -64,7 +64,6 @@
     parts = token_sems.shape[0]
     piece = length // parts
     r = lax.axis_index("dp")
-    m = lax.axis_index("mp")
 
     small = [
         pltpu.make_async_copy(src, dst, sems.at[i])
@@ -80,7 +79,7 @@
         )
         for i in range(parts)
     ]
-    for copy in small + pieces[:2] + weights + pieces[2:]:
+    for copy in small + pieces[:1] + weights + pieces[1:]:
         copy.start()
     small[2].wait()
 
@@ -180,11 +179,6 @@
 
     project(length // 2, length // 2)
 
-    seg_of = jnp.where(local < 0, slots, local)
-    member = jnp.where(seg == seg_of, 1.0, 0.0).astype(BF16)
-    columns = pl.ds(pl.multiple_of(m * width, width), width)
-    tok_ref[...] = jnp.dot(member, tokens_v[:, columns], preferred_element_type=F32)
-
     to_scalars.wait()
     def long(seg, start, end, reach):
         first = (start // 16) * 16
@@ -274,19 +268,24 @@
 
 
 def exchange_kernel(
-    dp, mp, q_ref, k_ref, v_ref, ctx_ref, tok_ref, bound_ref, meta_ref, target_ref, mass_ref, wo_hbm, cent_hbm,
+    dp, mp, q_ref, k_ref, v_ref, ctx_ref, bound_ref, meta_ref, target_ref, mass_ref,
+    wo_hbm, cent_hbm, tokens_hbm, ids_hbm,
     docs_ref, rows_ref, writes_ref, keep_ref,
     bound_s, ctx_s, part_s, carry_s, got_part, got_carry, tsend, tgot, ss_send, ss_got, csend, cgot, n_send, n_got,
-    wo_ref, cent_ref, ready, late_sems, bound_sem, part_sems, carry_sems, t_sems, ss_sems, c_sems, n_sems,
+    wo_ref, cent_ref, own_v, ids_v, ready, late_sems, bound_sem, part_sems, carry_sems, t_sems, ss_sems, c_sems, n_sems,
 ):
     r = lax.axis_index("dp")
     m = lax.axis_index("mp")
     slots = 32
     cents, width = cent_ref.shape
+    length = own_v.shape[0]
     load_wo = pltpu.make_async_copy(wo_hbm, wo_ref, late_sems.at[0])
     load_cent = pltpu.make_async_copy(cent_hbm, cent_ref, late_sems.at[1])
-    load_wo.start()
-    load_cent.start()
+    columns = pl.ds(pl.multiple_of(m * width, width), width)
+    load_own = pltpu.make_async_copy(tokens_hbm.at[:, columns], own_v, late_sems.at[2])
+    load_ids = pltpu.make_async_copy(ids_hbm, ids_v, late_sems.at[3])
+    for load in (load_ids, load_own, load_wo, load_cent):
+        load.start()
     to_scalars = pltpu.make_async_copy(bound_ref, bound_s, bound_sem)
     to_scalars.start()
 
@@ -312,7 +311,6 @@
 
     tsend[...] = target_ref[...].reshape(dp, 1, 128)
     tgot[0] = tsend[0]
-    ctx_s[slots + 1 :] = jnp.zeros((SEGS - slots - 1, 1, width), F32)
     to_scalars.wait()
     krow = iota((WIN, 1), 0)
     qlane = iota((1, 2 * WIN), 1) & (WIN - 1)
@@ -356,20 +354,26 @@
             low, wo_ref[...], preferred_element_type=F32
         )
 
-    @pl.loop(0, slots // GROUP)
+    before = slots // GROUP - 1
+
+    @pl.loop(0, before)
     def _(group):
         for j in range(GROUP):
             short(group * GROUP + j)
 
-    ctx_s[slots] = ctx_ref[slots]
+    load_ids.wait()
+    load_own.wait()
+    local = ids_v[...] - r * slots
+    member = jnp.where(iota((SEGS, length), 0) == jnp.where(local < 0, slots, local), 1.0, 0.0).astype(BF16)
+    tok = jnp.dot(member, own_v[...], preferred_element_type=F32)
+
     load_wo.wait()
-    projected = out_project(ctx_s[...].reshape(SEGS, width))
+    carried = out_project(ctx_ref[slots:].reshape(SEGS - slots, width))
     row8 = iota((8, width), 0)
     carried_count = meta_ref[8 + slots : 9 + slots, 0:1]
     for mm in range(mp):
-        block = projected[:, mm * width : (mm + 1) * width] + jnp.where(m == mm, tok_ref[...], 0.0)
-        part_s[mm] = block[:slots]
-        carry_s[mm] = jnp.where(row8 == 1, carried_count, block[slots:])
+        block = carried[:, mm * width : (mm + 1) * width] + jnp.where(m == mm, tok[slots:], 0.0)
+        carry_s[mm] = jnp.where(row8 == 1, carried_count, block)
 
     pl.semaphore_wait(barrier, mp - 1 + mp + layers - 1 + plane - 1)
     for mm in range(mp):
@@ -377,11 +381,17 @@
             src_ref=carry_s.at[mm], dst_ref=got_carry.at[m], send_sem=carry_sems.at[0],
             recv_sem=carry_sems.at[1], device_id=(prv, mm), device_id_type=MESH,
         ).start()
+    for i in range(1, layers):
+        pl.semaphore_signal(ready, inc=1, device_id=(along_z(i), m), device_id_type=MESH)
+
+    for j in range(GROUP):
+        short(before * GROUP + j)
+
+    projected = out_project(ctx_s[:slots].reshape(slots, width))
+    for mm in range(mp):
+        part_s[mm] = projected[:, mm * width : (mm + 1) * width] + jnp.where(m == mm, tok[:slots], 0.0)
     for dm in range(1, mp):
         to_peer(part_s.at[lax.rem(m + dm, mp)], got_part.at[mp - 1 - dm], part_sems, dm).start()
-
-    for i in range(1, layers):
-        pl.semaphore_signal(ready, inc=1, device_id=(along_z(i), m), device_id_type=MESH)
 
     d_wide = meta_ref[0:1, :]
     rank_wide = meta_ref[1:2, :]
@@ -531,13 +541,12 @@
     held = pl.pallas_call(
         rows_kernel,
         in_specs=[pl.BlockSpec(memory_space=pltpu.HBM)] * 7,
-        out_specs=[vmem] * 8,
+        out_specs=[vmem] * 7,
         out_shape=[
             shape(length // 16, 16, 2 * width, dtype=BF16),
             shape(length // 16, 16, width, dtype=BF16),
             shape(length // 16, 16, width, dtype=BF16),
             shape(SEGS, 1, width),
-            shape(SEGS, width),
             shape(SEGS, 128, dtype=jnp.int32),
             shape(8 + SEGS, 128),
             shape(dp, 128),
@@ -552,7 +561,7 @@
             pltpu.SMEM((SEGS, 128), jnp.int32),
             pltpu.VMEM((length + LONG, 2 * WIN), F32),
             pltpu.SemaphoreType.DMA((6,)),
-            pltpu.SemaphoreType.DMA((8,)),
+            pltpu.SemaphoreType.DMA((4,)),
             pltpu.SemaphoreType.DMA,
         ],
         compiler_params=pltpu.CompilerParams(vmem_limit_bytes=40 << 20),
@@ -566,7 +575,7 @@
     pair = pltpu.SemaphoreType.DMA((2,))
     new = pl.pallas_call(
         functools.partial(exchange_kernel, dp, mp),
-        in_specs=[vmem] * 9 + [pl.BlockSpec(memory_space=pl.ANY)] * 2,
+        in_specs=[vmem] * 8 + [pl.BlockSpec(memory_space=pl.ANY)] * 4,
         out_specs=[vmem] * 4,
         out_shape=[
             shape(slots, width),
@@ -576,7 +585,7 @@
         ],
         scratch_shapes=[
             pltpu.SMEM((SEGS, 128), jnp.int32),
-            pltpu.VMEM((SEGS, 1, width), F32),
+            pltpu.VMEM((slots, 1, width), F32),
             pltpu.VMEM((mp, slots, width), F32),
             pltpu.VMEM((mp, 8, width), F32),
             pltpu.VMEM((mp - 1, slots, width), F32),
@@ -591,8 +600,10 @@
             pltpu.VMEM((mp - 1, 8, 128), F32),
             pltpu.VMEM((width, D), BF16),
             pltpu.VMEM((cents, width), F32),
+            pltpu.VMEM((length, width), BF16),
+            pltpu.VMEM((1, length), jnp.int32),
             pltpu.SemaphoreType.REGULAR,
-            pltpu.SemaphoreType.DMA((2,)),
+            pltpu.SemaphoreType.DMA((4,)),
             pltpu.SemaphoreType.DMA,
             pair, pair, pair, pair, pair, pair,
         ],
@@ -601,7 +612,8 @@
         ),
         name="exchange",
     )(*held, cluster_mass.reshape(1, cents),
-        *[pltpu.with_memory_space_constraint(x, pltpu.HBM) for x in (w_out, centroids)])
+        *[pltpu.with_memory_space_constraint(x, pltpu.HBM)
+          for x in (w_out, centroids, tokens, doc_ids.reshape(1, length))])
 
     anywhere = pl.BlockSpec(memory_space=pl.ANY)
     return pl.pallas_call(

time: 42.4 us -> 42.9 us (1.012)
  Pallas kernels: 41.5 us -> 42 us
    pallas_call x1, Pallas kernels: 31.7 us -> 32.7 us  [shards(): pl.pallas_call(functools.partial(exchange_kernel, dp, mp), in_specs=[vmem...]
    pallas_call x1, Pallas kernels: 8.46 us -> 8 us  [shards(): pl.pallas_call(rows_kernel, in_specs=[pl.BlockSpec(memory_space=pltpu.HBM...]
where the time goes in v6:
time: 42.9 us
  Pallas kernels  42 us (98%)
  between operations  0.82 us (2%)
    pallas_call x1, Pallas kernels, shards(): pl.pallas_call(functools.partial(exchange_kernel, dp, mp), in_specs=[vmem...  32.7 us
    pallas_call x1, Pallas kernels, shards(): pl.pallas_call(rows_kernel, in_specs=[pl.BlockSpec(memory_space=pltpu.HBM...  8 us
    pallas_call x1, Pallas kernels, shards(): pl.pallas_call(write_kernel, in_specs=[vmem] * 4, out_specs=[anywhere] *...  1.29 us

profile of v6, /device:TPU:1, one launch (start us, length us, event | category | flops | bytes accessed | tf_op | source)
XLA Modules:
  0.0 42.9 jit_solution(4523051522336375410)
XLA Ops:
  0.6 0.0 copy-start
  0.6 8.0 %rows.1 = (bf16[128,16,512]{2,1,0:T(8,128)(2,1)S(1)}, bf16[128,16,256]{2,1,0:T(8,128)(2,1)S(1)}, bf16[128,16,256]{2,1,0:T(8,128)(2,1)S(1)}, f32[40,1,256]{2,1,0:...) custom-call(s32[1,2048]{1,0:T(1,128)} %bitcast.5, s32[1,32]{1,0:T(1,128)} %bitcast.8, ...), custom_call_target="tpu_custom_call" | custom-call | tf_op jit(solution)/shard_map/rows/pallas_call | solution.py:541
  8.6 0.0 copy-done
  8.7 32.7 %exchange.1 = (f32[32,256]{1,0:T(8,128)S(1)}, f32[128,256]{1,0:T(8,128)S(1)}, bf16[1024,128]{1,0:T(8,128)(2,1)S(1)}, f32[1024,256]{1,0:T(8,128)S(1)}) custom-call(bf16[128,16,512]{2,1,0:T(8,128)(2,1)S(1)} %get-tuple-element.13.q_ref, bf16[128,16,256]{2,1,0:T(8,128)(2,1)S(1)} %get-tuple-element.14.k_ref, bf16[128,16,256]{2,1,0:T(8,128)(2,1)S(1)} %get-tuple-element.15.v_ref, ...), custom_call_target="tpu_custom_call" | custom-call | tf_op jit(solution)/shard_map/exchange/pallas_call | solution.py:576
  41.4 1.3 %write.1 = (f32[32,256]{1,0:T(8,128)}, f32[1024,256]{1,0:T(8,128)}) custom-call(f32[32,256]{1,0:T(8,128)S(1)} %get-tuple-element.20.docs_ref, f32[128,256]{1,0:T(8,128)S(1)} %get-tuple-element.21.rows_ref, bf16[1024,128]{1,0:T(8,128)(2,1)S(1)} %get-tuple-element.22.writes_ref, f32[1024,256]{1,0:T(8,128)S(1)} %get-tuple-element.23.keep_ref), custom_call_target="tpu_custom_call" | custom-call | tf_op jit(solution)/shard_map/write/pallas_call | solution.py:619
Async XLA Ops:
  0.6 8.0 %copy-start = (f32[1024]{0:T(1024)S(1)}, f32[1024]{0:T(1024)}, u32[]{:S(2)}) copy-start(f32[1024]{0:T(1024)} %param.18) | copy-start | bytes 12292

commit v7 on v5

--- a/solution.py
+++ b/solution.py
@@ -13,7 +13,7 @@
 SEGS = 40
 WIN = 128
 LONG = 512
-GROUP = 16
+GROUP = 32
 F32 = jnp.float32
 BF16 = jnp.bfloat16
 MESH = pl.DeviceIdType.MESH
@@ -80,7 +80,7 @@
         )
         for i in range(parts)
     ]
-    for copy in small + pieces[:2] + weights + pieces[2:]:
+    for copy in small + pieces[:1] + weights + pieces[1:]:
         copy.start()
     small[2].wait()
 
@@ -552,7 +552,7 @@
             pltpu.SMEM((SEGS, 128), jnp.int32),
             pltpu.VMEM((length + LONG, 2 * WIN), F32),
             pltpu.SemaphoreType.DMA((6,)),
-            pltpu.SemaphoreType.DMA((8,)),
+            pltpu.SemaphoreType.DMA((4,)),
             pltpu.SemaphoreType.DMA,
         ],
         compiler_params=pltpu.CompilerParams(vmem_limit_bytes=40 << 20),

time: 42.4 us -> 42 us (level)
  Pallas kernels: 41.5 us -> 41 us
where the time goes in v7:
time: 42 us; the launch traced here: 41.8 us
  Pallas kernels  41 us (98%)
  between operations  0.82 us (2%)
    pallas_call x1, Pallas kernels, shards(): pl.pallas_call(functools.partial(exchange_kernel, dp, mp), in_specs=[vmem...  31.5 us
    pallas_call x1, Pallas kernels, shards(): pl.pallas_call(rows_kernel, in_specs=[pl.BlockSpec(memory_space=pltpu.HBM...  8.24 us
    pallas_call x1, Pallas kernels, shards(): pl.pallas_call(write_kernel, in_specs=[vmem] * 4, out_specs=[anywhere] *...  1.29 us

profile of v7, /device:TPU:1, one launch (start us, length us, event | category | flops | bytes accessed | tf_op | source)
XLA Modules:
  0.0 41.8 jit_solution(10227781126490481718)
XLA Ops:
  0.6 0.0 copy-start
  0.6 8.2 %rows.1 = (bf16[128,16,512]{2,1,0:T(8,128)(2,1)S(1)}, bf16[128,16,256]{2,1,0:T(8,128)(2,1)S(1)}, bf16[128,16,256]{2,1,0:T(8,128)(2,1)S(1)}, f32[40,1,256]{2,1,0:...) custom-call(s32[1,2048]{1,0:T(1,128)} %bitcast.5, ...), custom_call_target="tpu_custom_call" | custom-call | tf_op jit(solution)/shard_map/rows/pallas_call | solution.py:531
  8.9 0.0 copy-done
  8.9 31.5 %exchange.1 = (f32[32,256]{1,0:T(8,128)S(1)}, f32[128,256]{1,0:T(8,128)S(1)}, bf16[1024,128]{1,0:T(8,128)(2,1)S(1)}, f32[1024,256]{1,0:T(8,128)S(1)}) custom-call(bf16[128,16,512]{2,1,0:T(8,128)(2,1)S(1)} %get-tuple-element.14.q_ref, bf16[128,16,256]{2,1,0:T(8,128)(2,1)S(1)} %get-tuple-element.15.k_ref, bf16[128,16,256]{2,1,0:T(8,128)(2,1)S(1)} %get-tuple-element.16.v_ref, ...), custom_call_target="tpu_custom_call" | custom-call | tf_op jit(solution)/shard_map/exchange/pallas_call | solution.py:567
  40.4 1.3 %write.1 = (f32[32,256]{1,0:T(8,128)}, f32[1024,256]{1,0:T(8,128)}) custom-call(f32[32,256]{1,0:T(8,128)S(1)} %get-tuple-element.22.docs_ref, f32[128,256]{1,0:T(8,128)S(1)} %get-tuple-element.23.rows_ref, bf16[1024,128]{1,0:T(8,128)(2,1)S(1)} %get-tuple-element.24.writes_ref, f32[1024,256]{1,0:T(8,128)S(1)} %get-tuple-element.25.keep_ref), custom_call_target="tpu_custom_call" | custom-call | tf_op jit(solution)/shard_map/write/pallas_call | solution.py:607
Async XLA Ops:
  0.6 8.3 %copy-start = (f32[1024]{0:T(1024)S(1)}, f32[1024]{0:T(1024)}, u32[]{:S(2)}) copy-start(f32[1024]{0:T(1024)} %param.18) | copy-start | bytes 12292
